TPU v7x, 32 devices: a whole 2x2x4 slice. The times are simulated.
32 devices in a mesh: mesh: 8 (over z, x), sub: 4 (over y, core).
Axes of the slice: x: 2, y: 2, z: 4, core: 2. Of those that a mesh axis runs over, the one named last changes fastest.
Arguments:
- conductivity: float32 [4, 32, 2, 64, 128], P('sub', 'mesh'), may hold values from 0.3 to 3
- footprint: int32 [8, 8], replicated, may hold values from 0 to 31, as said below
- initial: float32 [8, 8, 512, 128], P('mesh', 'sub'), may hold values from -30 to 30
- observed: float32 [8, 3, 8, 512, 128], P('mesh', None, 'sub'), may hold values from -6 to 6
Outputs:
- gradient: float32 [4, 32, 2, 64, 128], P('sub', 'mesh')
- last_field: float32 [8, 8, 512, 128], P('mesh', 'sub')
Inputs may be any that keep to these rules, and one draw needn't show every extreme that they name: `footprint`: each row names 8 different blocks; in every row, each range k * 4 to (k + 1) * 4 - 1 holds at most one of the row's ids.
All inputs are finite; a program needn't handle non-finite values.
Results may differ from a plain program's by a relative error of at most 0.00011.
Values sent between devices are 32-bit elements; how exact they have to be, the bound alone decides.
A program may use at most 128 MiB of HBM per device.

v0:
```python
import jax
import jax.numpy as jnp
from jax import lax
from jax.sharding import PartitionSpec as P

STEPS = 3
DEG = 6
low_bound = 0.3
high_bound = 15.0


def padded_2(x, sides, width):
    for axis, dim in sides:
        count, length = (lax.axis_size(axis), x.shape[dim])
        up = [(i, (i + 1) % count) for i in range(count - 1)]
        down = [(j, i) for i, j in up]
        last = lax.slice_in_dim(x, length - width, length, axis=dim)
        leading = lax.slice_in_dim(x, 0, width, axis=dim)
        before = lax.ppermute(last, axis, up)
        after = lax.ppermute(leading, axis, down)
        x = jnp.concatenate([before, x, after], axis=dim)
    return x


def halo_operator(field, conduct):
    padded = padded_2(field, (("sub", 0),), 1)
    padded = jnp.pad(padded, ((0, 0), (1, 1), (1, 1)))
    beside = padded[2:, 1:-1, 1:-1] + padded[:-2, 1:-1, 1:-1]
    beside = beside + padded[1:-1, 2:, 1:-1] + padded[1:-1, :-2, 1:-1]
    beside = beside + padded[1:-1, 1:-1, 2:] + padded[1:-1, 1:-1, :-2]
    return (6.0 + conduct) * field - beside


def chebyshev(source, conduct, operate):
    centre = (high_bound + low_bound) / 2.0
    half_width = (high_bound - low_bound) / 2.0
    ratio_now = half_width / centre
    direct = source / centre
    remain = source
    iterate = direct
    for repeat in range(DEG):
        remain = remain - operate(direct, conduct)
        ratio_next = 1.0 / (2.0 * centre / half_width - ratio_now)
        direct = ratio_next * ratio_now * direct + 2.0 * ratio_next / half_width * remain
        iterate = iterate + direct
        ratio_now = ratio_next
    return iterate


def one_mesh(conduct, start_field, observed_mesh, operate):
    fields = [start_field]
    for step in range(STEPS):
        fields.append(chebyshev(conduct * fields[-1], conduct, operate))
    adjoint = jnp.zeros_like(start_field)
    summed = jnp.zeros_like(start_field)
    for step in range(STEPS, 0, -1):
        adjoint = chebyshev(
            fields[step] - observed_mesh[step - 1] + conduct * adjoint, conduct, operate
        )
        summed = summed + adjoint * (fields[step - 1] - fields[step])
    return (fields[-1], summed)


def body(conductivity, footprint, initial, observed):
    my_index = lax.axis_index("mesh")
    per_owner = conductivity.shape[1]
    depth = conductivity.shape[2]
    block_y = conductivity.shape[3]
    across = conductivity.shape[4]
    tile_count = footprint.shape[1]
    cell_count = depth * block_y * across
    my_blocks = lax.dynamic_index_in_dim(footprint, my_index, 0, keepdims=False)
    shard_rows = lax.all_gather(conductivity, "mesh", axis=1, tiled=True)
    row_count = shard_rows.shape[1]
    flat_rows = shard_rows[0].reshape(row_count, cell_count)
    chosen = (my_blocks[:, None] == jnp.arange(row_count, dtype=jnp.int32)[None, :]).astype(
        jnp.float32
    )
    tile_values = jnp.dot(chosen, flat_rows, precision=lax.Precision.HIGHEST)
    conduct = jnp.transpose(
        tile_values.reshape(tile_count, depth, block_y, across), (1, 0, 2, 3)
    ).reshape(depth, tile_count * block_y, across)
    final_field, summed = one_mesh(conduct, initial[0], observed[0], halo_operator)
    grad_tiles = jnp.transpose(
        summed.reshape(depth, tile_count, block_y, across), (1, 0, 2, 3)
    ).reshape(tile_count, cell_count)
    chosen = (
        jnp.arange(per_owner * lax.axis_size("mesh"), dtype=jnp.int32)[:, None]
        == my_blocks[None, :]
    ).astype(jnp.float32)
    grad_rows = lax.psum_scatter(
        jnp.dot(chosen, grad_tiles, precision=lax.Precision.HIGHEST),
        "mesh",
        scatter_dimension=0,
        tiled=True,
    )
    gradient = grad_rows.reshape(1, per_owner, depth, block_y, across)
    return (gradient, final_field[None])


def solution(mesh):
    return jax.shard_map(
        body,
        mesh=mesh,
        in_specs=(
            P("sub", "mesh", None, None, None),
            P(),
            P("mesh", "sub", None, None),
            P("mesh", None, "sub", None, None),
        ),
        out_specs=(P("sub", "mesh", None, None, None), P("mesh", "sub", None, None)),
        check_vma=False,
    )
```

profile of v0, /device:TPU:0, one launch (start us, length us, event | category | flops | bytes accessed | tf_op | source)
XLA Modules:
  0.0 570.4 jit_solution(3698757126698177843)
XLA Ops:
  8.0 54.2 %all-gather.2.cloned.1.call-done = f32[1,32,2,64,128]{4,3,2,0,1:T(8,128)} async-done(((f32[1,4,2,64,128]{4,3,2,0,1:T(8,128)}), f32[1,32,2,64,128]{4,3,2,0,1:T(8,128)}) %all-gather.2.cloned.1.call-update) | async-done | bytes 2097168 | tf_op jit(solution)/shard_map/all_gather | solution.py:73
  62.2 2.8 copy.27
  65.4 2.0 fusion.5
  68.9 3.0 collective-permute-start.1
  74.3 1.3 collective-permute-start.2
  75.6 5.8 %collective-permute-start.3 = (f32[1,512,128]{2,1,0:T(8,128)S(1)}, f32[1,512,128]{2,1,0:T(8,128)S(1)}, u32[]{:S(2)}, u32[]{:S(2)}) collective-permute-start(f32[1,512,128]{2,1,0:T(8,128)S(1)} %get-tuple-element.147), channel_id=1, source_target_pairs={{0,1},{1,2},{2,3},{4,5},{5,6},{6,7},{8,9},{9,10},{10,11},{12,13},{... | collective-permute-start | bytes 786440 | tf_op jit(solution)/shard_map/ppermute | solution.py:19
  83.7 1.3 collective-permute-start.4
  85.0 7.2 %collective-permute-start.5 = (f32[1,512,128]{2,1,0:T(8,128)S(1)}, f32[1,512,128]{2,1,0:T(8,128)S(1)}, u32[]{:S(2)}, u32[]{:S(2)}) collective-permute-start(f32[1,512,128]{2,1,0:T(8,128)S(1)} %get-tuple-element.145), channel_id=1, source_target_pairs={{0,1},{1,2},{2,3},{4,5},{5,6},{6,7},{8,9},{9,10},{10,11},{12,13},{... | collective-permute-start | bytes 786440 | tf_op jit(solution)/shard_map/ppermute | solution.py:19
  94.6 1.3 collective-permute-start.6
  95.9 7.2 %collective-permute-start.7 = (f32[1,512,128]{2,1,0:T(8,128)S(1)}, f32[1,512,128]{2,1,0:T(8,128)S(1)}, u32[]{:S(2)}, u32[]{:S(2)}) collective-permute-start(f32[1,512,128]{2,1,0:T(8,128)S(1)} %get-tuple-element.143), channel_id=1, source_target_pairs={{0,1},{1,2},{2,3},{4,5},{5,6},{6,7},{8,9},{9,10},{10,11},{12,13},{... | collective-permute-start | bytes 786440 | tf_op jit(solution)/shard_map/ppermute | solution.py:19
  106.7 7.2 %collective-permute-start.9 = (f32[1,512,128]{2,1,0:T(8,128)S(1)}, f32[1,512,128]{2,1,0:T(8,128)S(1)}, u32[]{:S(2)}, u32[]{:S(2)}) collective-permute-start(f32[1,512,128]{2,1,0:T(8,128)S(1)} %get-tuple-element.141), channel_id=1, source_target_pairs={{0,1},{1,2},{2,3},{4,5},{5,6},{6,7},{8,9},{9,10},{10,11},{12,13},{... | collective-permute-start | bytes 786440 | tf_op jit(solution)/shard_map/ppermute | solution.py:19
  117.5 7.4 %collective-permute-start.11 = (f32[1,512,128]{2,1,0:T(8,128)S(1)}, f32[1,512,128]{2,1,0:T(8,128)S(1)}, u32[]{:S(2)}, u32[]{:S(2)}) collective-permute-start(f32[1,512,128]{2,1,0:T(8,128)S(1)} %get-tuple-element.139), channel_id=1, source_target_pairs={{0,1},{1,2},{2,3},{4,5},{5,6},{6,7},{8,9},{9,10},{10,11},{12,13},{... | collective-permute-start | bytes 786440 | tf_op jit(solution)/shard_map/ppermute | solution.py:19
  128.5 7.2 %collective-permute-start.13 = (f32[1,512,128]{2,1,0:T(8,128)S(1)}, f32[1,512,128]{2,1,0:T(8,128)S(1)}, u32[]{:S(2)}, u32[]{:S(2)}) collective-permute-start(f32[1,512,128]{2,1,0:T(8,128)S(1)} %get-tuple-element.137), channel_id=1, source_target_pairs={{0,1},{1,2},{2,3},{4,5},{5,6},{6,7},{8,9},{9,10},{10,11},{12,13},{... | collective-permute-start | bytes 786440 | tf_op jit(solution)/shard_map/ppermute | solution.py:19
  139.3 7.2 %collective-permute-start.15 = (f32[1,512,128]{2,1,0:T(8,128)S(1)}, f32[1,512,128]{2,1,0:T(8,128)S(1)}, u32[]{:S(2)}, u32[]{:S(2)}) collective-permute-start(f32[1,512,128]{2,1,0:T(8,128)S(1)} %get-tuple-element.135), channel_id=1, source_target_pairs={{0,1},{1,2},{2,3},{4,5},{5,6},{6,7},{8,9},{9,10},{10,11},{12,13},{... | collective-permute-start | bytes 786440 | tf_op jit(solution)/shard_map/ppermute | solution.py:19
  148.8 1.3 collective-permute-start.16
  150.1 7.2 %collective-permute-start.17 = (f32[1,512,128]{2,1,0:T(8,128)S(1)}, f32[1,512,128]{2,1,0:T(8,128)S(1)}, u32[]{:S(2)}, u32[]{:S(2)}) collective-permute-start(f32[1,512,128]{2,1,0:T(8,128)S(1)} %get-tuple-element.133), channel_id=1, source_target_pairs={{0,1},{1,2},{2,3},{4,5},{5,6},{6,7},{8,9},{9,10},{10,11},{12,13},{... | collective-permute-start | bytes 786440 | tf_op jit(solution)/shard_map/ppermute | solution.py:19
  160.9 7.2 %collective-permute-start.19 = (f32[1,512,128]{2,1,0:T(8,128)S(1)}, f32[1,512,128]{2,1,0:T(8,128)S(1)}, u32[]{:S(2)}, u32[]{:S(2)}) collective-permute-start(f32[1,512,128]{2,1,0:T(8,128)S(1)} %get-tuple-element.131), channel_id=1, source_target_pairs={{0,1},{1,2},{2,3},{4,5},{5,6},{6,7},{8,9},{9,10},{10,11},{12,13},{... | collective-permute-start | bytes 786440 | tf_op jit(solution)/shard_map/ppermute | solution.py:19
  171.8 7.2 %collective-permute-start.21 = (f32[1,512,128]{2,1,0:T(8,128)S(1)}, f32[1,512,128]{2,1,0:T(8,128)S(1)}, u32[]{:S(2)}, u32[]{:S(2)}) collective-permute-start(f32[1,512,128]{2,1,0:T(8,128)S(1)} %get-tuple-element.129), channel_id=1, source_target_pairs={{0,1},{1,2},{2,3},{4,5},{5,6},{6,7},{8,9},{9,10},{10,11},{12,13},{... | collective-permute-start | bytes 786440 | tf_op jit(solution)/shard_map/ppermute | solution.py:19
  182.6 7.2 %collective-permute-start.23 = (f32[1,512,128]{2,1,0:T(8,128)S(1)}, f32[1,512,128]{2,1,0:T(8,128)S(1)}, u32[]{:S(2)}, u32[]{:S(2)}) collective-permute-start(f32[1,512,128]{2,1,0:T(8,128)S(1)} %get-tuple-element.127), channel_id=1, source_target_pairs={{0,1},{1,2},{2,3},{4,5},{5,6},{6,7},{8,9},{9,10},{10,11},{12,13},{... | collective-permute-start | bytes 786440 | tf_op jit(solution)/shard_map/ppermute | solution.py:19
  193.6 7.2 %collective-permute-start.25 = (f32[1,512,128]{2,1,0:T(8,128)S(1)}, f32[1,512,128]{2,1,0:T(8,128)S(1)}, u32[]{:S(2)}, u32[]{:S(2)}) collective-permute-start(f32[1,512,128]{2,1,0:T(8,128)S(1)} %get-tuple-element.125), channel_id=1, source_target_pairs={{0,1},{1,2},{2,3},{4,5},{5,6},{6,7},{8,9},{9,10},{10,11},{12,13},{... | collective-permute-start | bytes 786440 | tf_op jit(solution)/shard_map/ppermute | solution.py:19
  204.4 7.4 %collective-permute-start.27 = (f32[1,512,128]{2,1,0:T(8,128)S(1)}, f32[1,512,128]{2,1,0:T(8,128)S(1)}, u32[]{:S(2)}, u32[]{:S(2)}) collective-permute-start(f32[1,512,128]{2,1,0:T(8,128)S(1)} %get-tuple-element.123), channel_id=1, source_target_pairs={{0,1},{1,2},{2,3},{4,5},{5,6},{6,7},{8,9},{9,10},{10,11},{12,13},{... | collective-permute-start | bytes 786440 | tf_op jit(solution)/shard_map/ppermute | solution.py:19
  215.2 7.2 %collective-permute-start.29 = (f32[1,512,128]{2,1,0:T(8,128)S(1)}, f32[1,512,128]{2,1,0:T(8,128)S(1)}, u32[]{:S(2)}, u32[]{:S(2)}) collective-permute-start(f32[1,512,128]{2,1,0:T(8,128)S(1)} %get-tuple-element.121), channel_id=1, source_target_pairs={{0,1},{1,2},{2,3},{4,5},{5,6},{6,7},{8,9},{9,10},{10,11},{12,13},{... | collective-permute-start | bytes 786440 | tf_op jit(solution)/shard_map/ppermute | solution.py:19
  226.1 7.2 %collective-permute-start.31 = (f32[1,512,128]{2,1,0:T(8,128)S(1)}, f32[1,512,128]{2,1,0:T(8,128)S(1)}, u32[]{:S(2)}, u32[]{:S(2)}) collective-permute-start(f32[1,512,128]{2,1,0:T(8,128)S(1)} %get-tuple-element.119), channel_id=1, source_target_pairs={{0,1},{1,2},{2,3},{4,5},{5,6},{6,7},{8,9},{9,10},{10,11},{12,13},{... | collective-permute-start | bytes 786440 | tf_op jit(solution)/shard_map/ppermute | solution.py:19
  236.9 7.2 %collective-permute-start.33 = (f32[1,512,128]{2,1,0:T(8,128)S(1)}, f32[1,512,128]{2,1,0:T(8,128)S(1)}, u32[]{:S(2)}, u32[]{:S(2)}) collective-permute-start(f32[1,512,128]{2,1,0:T(8,128)S(1)} %get-tuple-element.117), channel_id=1, source_target_pairs={{0,1},{1,2},{2,3},{4,5},{5,6},{6,7},{8,9},{9,10},{10,11},{12,13},{... | collective-permute-start | bytes 786440 | tf_op jit(solution)/shard_map/ppermute | solution.py:19
  246.4 1.4 collective-permute-start.34
  247.8 7.2 %collective-permute-start.35 = (f32[1,512,128]{2,1,0:T(8,128)S(1)}, f32[1,512,128]{2,1,0:T(8,128)S(1)}, u32[]{:S(2)}, u32[]{:S(2)}) collective-permute-start(f32[1,512,128]{2,1,0:T(8,128)S(1)} %get-tuple-element.115), channel_id=1, source_target_pairs={{0,1},{1,2},{2,3},{4,5},{5,6},{6,7},{8,9},{9,10},{10,11},{12,13},{... | collective-permute-start | bytes 786440 | tf_op jit(solution)/shard_map/ppermute | solution.py:19
  258.8 7.2 %collective-permute-start.37 = (f32[1,512,128]{2,1,0:T(8,128)S(1)}, f32[1,512,128]{2,1,0:T(8,128)S(1)}, u32[]{:S(2)}, u32[]{:S(2)}) collective-permute-start(f32[1,512,128]{2,1,0:T(8,128)S(1)} %get-tuple-element.113), channel_id=1, source_target_pairs={{0,1},{1,2},{2,3},{4,5},{5,6},{6,7},{8,9},{9,10},{10,11},{12,13},{... | collective-permute-start | bytes 786440 | tf_op jit(solution)/shard_map/ppermute | solution.py:19
  269.7 7.2 %collective-permute-start.39 = (f32[1,512,128]{2,1,0:T(8,128)S(1)}, f32[1,512,128]{2,1,0:T(8,128)S(1)}, u32[]{:S(2)}, u32[]{:S(2)}) collective-permute-start(f32[1,512,128]{2,1,0:T(8,128)S(1)} %get-tuple-element.111), channel_id=1, source_target_pairs={{0,1},{1,2},{2,3},{4,5},{5,6},{6,7},{8,9},{9,10},{10,11},{12,13},{... | collective-permute-start | bytes 786440 | tf_op jit(solution)/shard_map/ppermute | solution.py:19
  279.2 1.3 collective-permute-start.40
  280.5 7.2 %collective-permute-start.41 = (f32[1,512,128]{2,1,0:T(8,128)S(1)}, f32[1,512,128]{2,1,0:T(8,128)S(1)}, u32[]{:S(2)}, u32[]{:S(2)}) collective-permute-start(f32[1,512,128]{2,1,0:T(8,128)S(1)} %get-tuple-element.109), channel_id=1, source_target_pairs={{0,1},{1,2},{2,3},{4,5},{5,6},{6,7},{8,9},{9,10},{10,11},{12,13},{... | collective-permute-start | bytes 786440 | tf_op jit(solution)/shard_map/ppermute | solution.py:19
  290.0 1.3 collective-permute-start.42
  291.3 7.6 %collective-permute-start.43 = (f32[1,512,128]{2,1,0:T(8,128)S(1)}, f32[1,512,128]{2,1,0:T(8,128)S(1)}, u32[]{:S(2)}, u32[]{:S(2)}) collective-permute-start(f32[1,512,128]{2,1,0:T(8,128)S(1)} %get-tuple-element.107), channel_id=1, source_target_pairs={{0,1},{1,2},{2,3},{4,5},{5,6},{6,7},{8,9},{9,10},{10,11},{12,13},{... | collective-permute-start | bytes 786440 | tf_op jit(solution)/shard_map/ppermute | solution.py:19
  302.1 7.2 %collective-permute-start.45 = (f32[1,512,128]{2,1,0:T(8,128)S(1)}, f32[1,512,128]{2,1,0:T(8,128)S(1)}, u32[]{:S(2)}, u32[]{:S(2)}) collective-permute-start(f32[1,512,128]{2,1,0:T(8,128)S(1)} %get-tuple-element.105), channel_id=1, source_target_pairs={{0,1},{1,2},{2,3},{4,5},{5,6},{6,7},{8,9},{9,10},{10,11},{12,13},{... | collective-permute-start | bytes 786440 | tf_op jit(solution)/shard_map/ppermute | solution.py:19
  312.9 7.2 %collective-permute-start.47 = (f32[1,512,128]{2,1,0:T(8,128)S(1)}, f32[1,512,128]{2,1,0:T(8,128)S(1)}, u32[]{:S(2)}, u32[]{:S(2)}) collective-permute-start(f32[1,512,128]{2,1,0:T(8,128)S(1)} %get-tuple-element.103), channel_id=1, source_target_pairs={{0,1},{1,2},{2,3},{4,5},{5,6},{6,7},{8,9},{9,10},{10,11},{12,13},{... | collective-permute-start | bytes 786440 | tf_op jit(solution)/shard_map/ppermute | solution.py:19
  324.0 7.2 %collective-permute-start.49 = (f32[1,512,128]{2,1,0:T(8,128)S(1)}, f32[1,512,128]{2,1,0:T(8,128)S(1)}, u32[]{:S(2)}, u32[]{:S(2)}) collective-permute-start(f32[1,512,128]{2,1,0:T(8,128)S(1)} %get-tuple-element.101), channel_id=1, source_target_pairs={{0,1},{1,2},{2,3},{4,5},{5,6},{6,7},{8,9},{9,10},{10,11},{12,13},{... | collective-permute-start | bytes 786440 | tf_op jit(solution)/shard_map/ppermute | solution.py:19
  334.8 7.2 %collective-permute-start.51 = (f32[1,512,128]{2,1,0:T(8,128)S(1)}, f32[1,512,128]{2,1,0:T(8,128)S(1)}, u32[]{:S(2)}, u32[]{:S(2)}) collective-permute-start(f32[1,512,128]{2,1,0:T(8,128)S(1)} %get-tuple-element.99), channel_id=1, source_target_pairs={{0,1},{1,2},{2,3},{4,5},{5,6},{6,7},{8,9},{9,10},{10,11},{12,13},{... | collective-permute-start | bytes 786440 | tf_op jit(solution)/shard_map/ppermute | solution.py:19
  345.6 7.2 %collective-permute-start.53 = (f32[1,512,128]{2,1,0:T(8,128)S(1)}, f32[1,512,128]{2,1,0:T(8,128)S(1)}, u32[]{:S(2)}, u32[]{:S(2)}) collective-permute-start(f32[1,512,128]{2,1,0:T(8,128)S(1)} %get-tuple-element.97), channel_id=1, source_target_pairs={{0,1},{1,2},{2,3},{4,5},{5,6},{6,7},{8,9},{9,10},{10,11},{12,13},{... | collective-permute-start | bytes 786440 | tf_op jit(solution)/shard_map/ppermute | solution.py:19
  356.4 7.2 %collective-permute-start.55 = (f32[1,512,128]{2,1,0:T(8,128)S(1)}, f32[1,512,128]{2,1,0:T(8,128)S(1)}, u32[]{:S(2)}, u32[]{:S(2)}) collective-permute-start(f32[1,512,128]{2,1,0:T(8,128)S(1)} %get-tuple-element.95), channel_id=1, source_target_pairs={{0,1},{1,2},{2,3},{4,5},{5,6},{6,7},{8,9},{9,10},{10,11},{12,13},{... | collective-permute-start | bytes 786440 | tf_op jit(solution)/shard_map/ppermute | solution.py:19
  367.2 7.2 %collective-permute-start.57 = (f32[1,512,128]{2,1,0:T(8,128)S(1)}, f32[1,512,128]{2,1,0:T(8,128)S(1)}, u32[]{:S(2)}, u32[]{:S(2)}) collective-permute-start(f32[1,512,128]{2,1,0:T(8,128)S(1)} %get-tuple-element.93), channel_id=1, source_target_pairs={{0,1},{1,2},{2,3},{4,5},{5,6},{6,7},{8,9},{9,10},{10,11},{12,13},{... | collective-permute-start | bytes 786440 | tf_op jit(solution)/shard_map/ppermute | solution.py:19
  378.0 7.4 %collective-permute-start.59 = (f32[1,512,128]{2,1,0:T(8,128)S(1)}, f32[1,512,128]{2,1,0:T(8,128)S(1)}, u32[]{:S(2)}, u32[]{:S(2)}) collective-permute-start(f32[1,512,128]{2,1,0:T(8,128)S(1)} %get-tuple-element.91), channel_id=1, source_target_pairs={{0,1},{1,2},{2,3},{4,5},{5,6},{6,7},{8,9},{9,10},{10,11},{12,13},{... | collective-permute-start | bytes 786440 | tf_op jit(solution)/shard_map/ppermute | solution.py:19
  389.1 7.2 %collective-permute-start.61 = (f32[1,512,128]{2,1,0:T(8,128)S(1)}, f32[1,512,128]{2,1,0:T(8,128)S(1)}, u32[]{:S(2)}, u32[]{:S(2)}) collective-permute-start(f32[1,512,128]{2,1,0:T(8,128)S(1)} %get-tuple-element.89), channel_id=1, source_target_pairs={{0,1},{1,2},{2,3},{4,5},{5,6},{6,7},{8,9},{9,10},{10,11},{12,13},{... | collective-permute-start | bytes 786440 | tf_op jit(solution)/shard_map/ppermute | solution.py:19
  399.9 7.2 %collective-permute-start.63 = (f32[1,512,128]{2,1,0:T(8,128)S(1)}, f32[1,512,128]{2,1,0:T(8,128)S(1)}, u32[]{:S(2)}, u32[]{:S(2)}) collective-permute-start(f32[1,512,128]{2,1,0:T(8,128)S(1)} %get-tuple-element.87), channel_id=1, source_target_pairs={{0,1},{1,2},{2,3},{4,5},{5,6},{6,7},{8,9},{9,10},{10,11},{12,13},{... | collective-permute-start | bytes 786440 | tf_op jit(solution)/shard_map/ppermute | solution.py:19
  410.7 7.2 %collective-permute-start.65 = (f32[1,512,128]{2,1,0:T(8,128)S(1)}, f32[1,512,128]{2,1,0:T(8,128)S(1)}, u32[]{:S(2)}, u32[]{:S(2)}) collective-permute-start(f32[1,512,128]{2,1,0:T(8,128)S(1)} %get-tuple-element.85), channel_id=1, source_target_pairs={{0,1},{1,2},{2,3},{4,5},{5,6},{6,7},{8,9},{9,10},{10,11},{12,13},{... | collective-permute-start | bytes 786440 | tf_op jit(solution)/shard_map/ppermute | solution.py:19
  421.5 7.2 %collective-permute-start.67 = (f32[1,512,128]{2,1,0:T(8,128)S(1)}, f32[1,512,128]{2,1,0:T(8,128)S(1)}, u32[]{:S(2)}, u32[]{:S(2)}) collective-permute-start(f32[1,512,128]{2,1,0:T(8,128)S(1)} %get-tuple-element.83), channel_id=1, source_target_pairs={{0,1},{1,2},{2,3},{4,5},{5,6},{6,7},{8,9},{9,10},{10,11},{12,13},{... | collective-permute-start | bytes 786440 | tf_op jit(solution)/shard_map/ppermute | solution.py:19
  432.3 7.2 %collective-permute-start.69 = (f32[1,512,128]{2,1,0:T(8,128)S(1)}, f32[1,512,128]{2,1,0:T(8,128)S(1)}, u32[]{:S(2)}, u32[]{:S(2)}) collective-permute-start(f32[1,512,128]{2,1,0:T(8,128)S(1)} %get-tuple-element.81), channel_id=1, source_target_pairs={{0,1},{1,2},{2,3},{4,5},{5,6},{6,7},{8,9},{9,10},{10,11},{12,13},{... | collective-permute-start | bytes 786440 | tf_op jit(solution)/shard_map/ppermute | solution.py:19
  443.1 7.2 %collective-permute-start.71 = (f32[1,512,128]{2,1,0:T(8,128)S(1)}, f32[1,512,128]{2,1,0:T(8,128)S(1)}, u32[]{:S(2)}, u32[]{:S(2)}) collective-permute-start(f32[1,512,128]{2,1,0:T(8,128)S(1)} %get-tuple-element.79), channel_id=1, source_target_pairs={{0,1},{1,2},{2,3},{4,5},{5,6},{6,7},{8,9},{9,10},{10,11},{12,13},{... | collective-permute-start | bytes 786440 | tf_op jit(solution)/shard_map/ppermute | solution.py:19
  453.1 2.4 fusion.8
  456.7 104.8 %all-reduce.39.cloned.1.call-done = f32[32,16384]{1,0:T(8,128)} async-done(((f32[32,16384]{1,0:T(8,128)}), f32[32,16384]{1,0:T(8,128)}) %all-reduce.39.cloned.1.call-update) | async-done | bytes 2097168
  (233 shorter events, 124.3 us)
Async XLA Ops:
  7.2 55.0 %all-gather.2.cloned.1.call-start = ((), (), s32[]{:S(2)}) async-start(), calls=%async_computation | async-start | bytes 2359296 | tf_op jit(solution)/shard_map/all_gather | solution.py:73
  7.9 553.6 %all-reduce.39.cloned.1.call-start = ((), (), s32[]{:S(2)}) async-start(), calls=%async_computation.1 | async-start | bytes 4194304
  83.7 8.5 %collective-permute-start.4 = (f32[1,512,128]{2,1,0:T(8,128)S(1)}, f32[1,512,128]{2,1,0:T(8,128)S(1)}, u32[]{:S(2)}, u32[]{:S(2)}) collective-permute-start(f32[1,512,128]{2,1,0:T(8,128)S(1)} %get-tuple-element.146), channel_id=1, source_target_pairs={{1,0},{2,1},{3,2},{5,4},{6,5},{7,6},{9,8},{10,9},{11,10},{13,12},{... | collective-permute-start | bytes 786440 | tf_op jit(solution)/shard_map/ppermute | solution.py:20
  85.0 8.3 %collective-permute-start.5 = (f32[1,512,128]{2,1,0:T(8,128)S(1)}, f32[1,512,128]{2,1,0:T(8,128)S(1)}, u32[]{:S(2)}, u32[]{:S(2)}) collective-permute-start(f32[1,512,128]{2,1,0:T(8,128)S(1)} %get-tuple-element.145), channel_id=1, source_target_pairs={{0,1},{1,2},{2,3},{4,5},{5,6},{6,7},{8,9},{9,10},{10,11},{12,13},{... | collective-permute-start | bytes 786440 | tf_op jit(solution)/shard_map/ppermute | solution.py:19
  94.6 8.5 %collective-permute-start.6 = (f32[1,512,128]{2,1,0:T(8,128)S(1)}, f32[1,512,128]{2,1,0:T(8,128)S(1)}, u32[]{:S(2)}, u32[]{:S(2)}) collective-permute-start(f32[1,512,128]{2,1,0:T(8,128)S(1)} %get-tuple-element.144), channel_id=1, source_target_pairs={{1,0},{2,1},{3,2},{5,4},{6,5},{7,6},{9,8},{10,9},{11,10},{13,12},{... | collective-permute-start | bytes 786440 | tf_op jit(solution)/shard_map/ppermute | solution.py:20
  95.9 8.3 %collective-permute-start.7 = (f32[1,512,128]{2,1,0:T(8,128)S(1)}, f32[1,512,128]{2,1,0:T(8,128)S(1)}, u32[]{:S(2)}, u32[]{:S(2)}) collective-permute-start(f32[1,512,128]{2,1,0:T(8,128)S(1)} %get-tuple-element.143), channel_id=1, source_target_pairs={{0,1},{1,2},{2,3},{4,5},{5,6},{6,7},{8,9},{9,10},{10,11},{12,13},{... | collective-permute-start | bytes 786440 | tf_op jit(solution)/shard_map/ppermute | solution.py:19
  105.4 8.5 %collective-permute-start.8 = (f32[1,512,128]{2,1,0:T(8,128)S(1)}, f32[1,512,128]{2,1,0:T(8,128)S(1)}, u32[]{:S(2)}, u32[]{:S(2)}) collective-permute-start(f32[1,512,128]{2,1,0:T(8,128)S(1)} %get-tuple-element.142), channel_id=1, source_target_pairs={{1,0},{2,1},{3,2},{5,4},{6,5},{7,6},{9,8},{10,9},{11,10},{13,12},{... | collective-permute-start | bytes 786440 | tf_op jit(solution)/shard_map/ppermute | solution.py:20
  106.7 8.3 %collective-permute-start.9 = (f32[1,512,128]{2,1,0:T(8,128)S(1)}, f32[1,512,128]{2,1,0:T(8,128)S(1)}, u32[]{:S(2)}, u32[]{:S(2)}) collective-permute-start(f32[1,512,128]{2,1,0:T(8,128)S(1)} %get-tuple-element.141), channel_id=1, source_target_pairs={{0,1},{1,2},{2,3},{4,5},{5,6},{6,7},{8,9},{9,10},{10,11},{12,13},{... | collective-permute-start | bytes 786440 | tf_op jit(solution)/shard_map/ppermute | solution.py:19
  116.2 8.7 %collective-permute-start.10 = (f32[1,512,128]{2,1,0:T(8,128)S(1)}, f32[1,512,128]{2,1,0:T(8,128)S(1)}, u32[]{:S(2)}, u32[]{:S(2)}) collective-permute-start(f32[1,512,128]{2,1,0:T(8,128)S(1)} %get-tuple-element.140), channel_id=1, source_target_pairs={{1,0},{2,1},{3,2},{5,4},{6,5},{7,6},{9,8},{10,9},{11,10},{13,12},{... | collective-permute-start | bytes 786440 | tf_op jit(solution)/shard_map/ppermute | solution.py:20
  117.5 8.3 %collective-permute-start.11 = (f32[1,512,128]{2,1,0:T(8,128)S(1)}, f32[1,512,128]{2,1,0:T(8,128)S(1)}, u32[]{:S(2)}, u32[]{:S(2)}) collective-permute-start(f32[1,512,128]{2,1,0:T(8,128)S(1)} %get-tuple-element.139), channel_id=1, source_target_pairs={{0,1},{1,2},{2,3},{4,5},{5,6},{6,7},{8,9},{9,10},{10,11},{12,13},{... | collective-permute-start | bytes 786440 | tf_op jit(solution)/shard_map/ppermute | solution.py:19
  127.2 8.5 %collective-permute-start.12 = (f32[1,512,128]{2,1,0:T(8,128)S(1)}, f32[1,512,128]{2,1,0:T(8,128)S(1)}, u32[]{:S(2)}, u32[]{:S(2)}) collective-permute-start(f32[1,512,128]{2,1,0:T(8,128)S(1)} %get-tuple-element.138), channel_id=1, source_target_pairs={{1,0},{2,1},{3,2},{5,4},{6,5},{7,6},{9,8},{10,9},{11,10},{13,12},{... | collective-permute-start | bytes 786440 | tf_op jit(solution)/shard_map/ppermute | solution.py:20
  128.5 8.3 %collective-permute-start.13 = (f32[1,512,128]{2,1,0:T(8,128)S(1)}, f32[1,512,128]{2,1,0:T(8,128)S(1)}, u32[]{:S(2)}, u32[]{:S(2)}) collective-permute-start(f32[1,512,128]{2,1,0:T(8,128)S(1)} %get-tuple-element.137), channel_id=1, source_target_pairs={{0,1},{1,2},{2,3},{4,5},{5,6},{6,7},{8,9},{9,10},{10,11},{12,13},{... | collective-permute-start | bytes 786440 | tf_op jit(solution)/shard_map/ppermute | solution.py:19
  138.0 8.5 %collective-permute-start.14 = (f32[1,512,128]{2,1,0:T(8,128)S(1)}, f32[1,512,128]{2,1,0:T(8,128)S(1)}, u32[]{:S(2)}, u32[]{:S(2)}) collective-permute-start(f32[1,512,128]{2,1,0:T(8,128)S(1)} %get-tuple-element.136), channel_id=1, source_target_pairs={{1,0},{2,1},{3,2},{5,4},{6,5},{7,6},{9,8},{10,9},{11,10},{13,12},{... | collective-permute-start | bytes 786440 | tf_op jit(solution)/shard_map/ppermute | solution.py:20
  139.3 8.3 %collective-permute-start.15 = (f32[1,512,128]{2,1,0:T(8,128)S(1)}, f32[1,512,128]{2,1,0:T(8,128)S(1)}, u32[]{:S(2)}, u32[]{:S(2)}) collective-permute-start(f32[1,512,128]{2,1,0:T(8,128)S(1)} %get-tuple-element.135), channel_id=1, source_target_pairs={{0,1},{1,2},{2,3},{4,5},{5,6},{6,7},{8,9},{9,10},{10,11},{12,13},{... | collective-permute-start | bytes 786440 | tf_op jit(solution)/shard_map/ppermute | solution.py:19
  148.8 8.5 %collective-permute-start.16 = (f32[1,512,128]{2,1,0:T(8,128)S(1)}, f32[1,512,128]{2,1,0:T(8,128)S(1)}, u32[]{:S(2)}, u32[]{:S(2)}) collective-permute-start(f32[1,512,128]{2,1,0:T(8,128)S(1)} %get-tuple-element.134), channel_id=1, source_target_pairs={{1,0},{2,1},{3,2},{5,4},{6,5},{7,6},{9,8},{10,9},{11,10},{13,12},{... | collective-permute-start | bytes 786440 | tf_op jit(solution)/shard_map/ppermute | solution.py:20
  150.1 8.3 %collective-permute-start.17 = (f32[1,512,128]{2,1,0:T(8,128)S(1)}, f32[1,512,128]{2,1,0:T(8,128)S(1)}, u32[]{:S(2)}, u32[]{:S(2)}) collective-permute-start(f32[1,512,128]{2,1,0:T(8,128)S(1)} %get-tuple-element.133), channel_id=1, source_target_pairs={{0,1},{1,2},{2,3},{4,5},{5,6},{6,7},{8,9},{9,10},{10,11},{12,13},{... | collective-permute-start | bytes 786440 | tf_op jit(solution)/shard_map/ppermute | solution.py:19
  159.6 8.5 %collective-permute-start.18 = (f32[1,512,128]{2,1,0:T(8,128)S(1)}, f32[1,512,128]{2,1,0:T(8,128)S(1)}, u32[]{:S(2)}, u32[]{:S(2)}) collective-permute-start(f32[1,512,128]{2,1,0:T(8,128)S(1)} %get-tuple-element.132), channel_id=1, source_target_pairs={{1,0},{2,1},{3,2},{5,4},{6,5},{7,6},{9,8},{10,9},{11,10},{13,12},{... | collective-permute-start | bytes 786440 | tf_op jit(solution)/shard_map/ppermute | solution.py:20
  160.9 8.3 %collective-permute-start.19 = (f32[1,512,128]{2,1,0:T(8,128)S(1)}, f32[1,512,128]{2,1,0:T(8,128)S(1)}, u32[]{:S(2)}, u32[]{:S(2)}) collective-permute-start(f32[1,512,128]{2,1,0:T(8,128)S(1)} %get-tuple-element.131), channel_id=1, source_target_pairs={{0,1},{1,2},{2,3},{4,5},{5,6},{6,7},{8,9},{9,10},{10,11},{12,13},{... | collective-permute-start | bytes 786440 | tf_op jit(solution)/shard_map/ppermute | solution.py:19
  170.5 8.5 %collective-permute-start.20 = (f32[1,512,128]{2,1,0:T(8,128)S(1)}, f32[1,512,128]{2,1,0:T(8,128)S(1)}, u32[]{:S(2)}, u32[]{:S(2)}) collective-permute-start(f32[1,512,128]{2,1,0:T(8,128)S(1)} %get-tuple-element.130), channel_id=1, source_target_pairs={{1,0},{2,1},{3,2},{5,4},{6,5},{7,6},{9,8},{10,9},{11,10},{13,12},{... | collective-permute-start | bytes 786440 | tf_op jit(solution)/shard_map/ppermute | solution.py:20
  171.8 8.3 %collective-permute-start.21 = (f32[1,512,128]{2,1,0:T(8,128)S(1)}, f32[1,512,128]{2,1,0:T(8,128)S(1)}, u32[]{:S(2)}, u32[]{:S(2)}) collective-permute-start(f32[1,512,128]{2,1,0:T(8,128)S(1)} %get-tuple-element.129), channel_id=1, source_target_pairs={{0,1},{1,2},{2,3},{4,5},{5,6},{6,7},{8,9},{9,10},{10,11},{12,13},{... | collective-permute-start | bytes 786440 | tf_op jit(solution)/shard_map/ppermute | solution.py:19
  181.3 8.5 %collective-permute-start.22 = (f32[1,512,128]{2,1,0:T(8,128)S(1)}, f32[1,512,128]{2,1,0:T(8,128)S(1)}, u32[]{:S(2)}, u32[]{:S(2)}) collective-permute-start(f32[1,512,128]{2,1,0:T(8,128)S(1)} %get-tuple-element.128), channel_id=1, source_target_pairs={{1,0},{2,1},{3,2},{5,4},{6,5},{7,6},{9,8},{10,9},{11,10},{13,12},{... | collective-permute-start | bytes 786440 | tf_op jit(solution)/shard_map/ppermute | solution.py:20
  182.6 8.3 %collective-permute-start.23 = (f32[1,512,128]{2,1,0:T(8,128)S(1)}, f32[1,512,128]{2,1,0:T(8,128)S(1)}, u32[]{:S(2)}, u32[]{:S(2)}) collective-permute-start(f32[1,512,128]{2,1,0:T(8,128)S(1)} %get-tuple-element.127), channel_id=1, source_target_pairs={{0,1},{1,2},{2,3},{4,5},{5,6},{6,7},{8,9},{9,10},{10,11},{12,13},{... | collective-permute-start | bytes 786440 | tf_op jit(solution)/shard_map/ppermute | solution.py:19
  192.3 8.5 %collective-permute-start.24 = (f32[1,512,128]{2,1,0:T(8,128)S(1)}, f32[1,512,128]{2,1,0:T(8,128)S(1)}, u32[]{:S(2)}, u32[]{:S(2)}) collective-permute-start(f32[1,512,128]{2,1,0:T(8,128)S(1)} %get-tuple-element.126), channel_id=1, source_target_pairs={{1,0},{2,1},{3,2},{5,4},{6,5},{7,6},{9,8},{10,9},{11,10},{13,12},{... | collective-permute-start | bytes 786440 | tf_op jit(solution)/shard_map/ppermute | solution.py:20
  193.6 8.3 %collective-permute-start.25 = (f32[1,512,128]{2,1,0:T(8,128)S(1)}, f32[1,512,128]{2,1,0:T(8,128)S(1)}, u32[]{:S(2)}, u32[]{:S(2)}) collective-permute-start(f32[1,512,128]{2,1,0:T(8,128)S(1)} %get-tuple-element.125), channel_id=1, source_target_pairs={{0,1},{1,2},{2,3},{4,5},{5,6},{6,7},{8,9},{9,10},{10,11},{12,13},{... | collective-permute-start | bytes 786440 | tf_op jit(solution)/shard_map/ppermute | solution.py:19
  203.1 8.7 %collective-permute-start.26 = (f32[1,512,128]{2,1,0:T(8,128)S(1)}, f32[1,512,128]{2,1,0:T(8,128)S(1)}, u32[]{:S(2)}, u32[]{:S(2)}) collective-permute-start(f32[1,512,128]{2,1,0:T(8,128)S(1)} %get-tuple-element.124), channel_id=1, source_target_pairs={{1,0},{2,1},{3,2},{5,4},{6,5},{7,6},{9,8},{10,9},{11,10},{13,12},{... | collective-permute-start | bytes 786440 | tf_op jit(solution)/shard_map/ppermute | solution.py:20
  204.4 8.3 %collective-permute-start.27 = (f32[1,512,128]{2,1,0:T(8,128)S(1)}, f32[1,512,128]{2,1,0:T(8,128)S(1)}, u32[]{:S(2)}, u32[]{:S(2)}) collective-permute-start(f32[1,512,128]{2,1,0:T(8,128)S(1)} %get-tuple-element.123), channel_id=1, source_target_pairs={{0,1},{1,2},{2,3},{4,5},{5,6},{6,7},{8,9},{9,10},{10,11},{12,13},{... | collective-permute-start | bytes 786440 | tf_op jit(solution)/shard_map/ppermute | solution.py:19
  213.9 8.5 %collective-permute-start.28 = (f32[1,512,128]{2,1,0:T(8,128)S(1)}, f32[1,512,128]{2,1,0:T(8,128)S(1)}, u32[]{:S(2)}, u32[]{:S(2)}) collective-permute-start(f32[1,512,128]{2,1,0:T(8,128)S(1)} %get-tuple-element.122), channel_id=1, source_target_pairs={{1,0},{2,1},{3,2},{5,4},{6,5},{7,6},{9,8},{10,9},{11,10},{13,12},{... | collective-permute-start | bytes 786440 | tf_op jit(solution)/shard_map/ppermute | solution.py:20
  224.8 8.5 %collective-permute-start.30 = (f32[1,512,128]{2,1,0:T(8,128)S(1)}, f32[1,512,128]{2,1,0:T(8,128)S(1)}, u32[]{:S(2)}, u32[]{:S(2)}) collective-permute-start(f32[1,512,128]{2,1,0:T(8,128)S(1)} %get-tuple-element.120), channel_id=1, source_target_pairs={{1,0},{2,1},{3,2},{5,4},{6,5},{7,6},{9,8},{10,9},{11,10},{13,12},{... | collective-permute-start | bytes 786440 | tf_op jit(solution)/shard_map/ppermute | solution.py:20
  235.6 8.5 %collective-permute-start.32 = (f32[1,512,128]{2,1,0:T(8,128)S(1)}, f32[1,512,128]{2,1,0:T(8,128)S(1)}, u32[]{:S(2)}, u32[]{:S(2)}) collective-permute-start(f32[1,512,128]{2,1,0:T(8,128)S(1)} %get-tuple-element.118), channel_id=1, source_target_pairs={{1,0},{2,1},{3,2},{5,4},{6,5},{7,6},{9,8},{10,9},{11,10},{13,12},{... | collective-permute-start | bytes 786440 | tf_op jit(solution)/shard_map/ppermute | solution.py:20
  246.4 8.6 %collective-permute-start.34 = (f32[1,512,128]{2,1,0:T(8,128)S(1)}, f32[1,512,128]{2,1,0:T(8,128)S(1)}, u32[]{:S(2)}, u32[]{:S(2)}) collective-permute-start(f32[1,512,128]{2,1,0:T(8,128)S(1)} %get-tuple-element.116), channel_id=1, source_target_pairs={{1,0},{2,1},{3,2},{5,4},{6,5},{7,6},{9,8},{10,9},{11,10},{13,12},{... | collective-permute-start | bytes 786440 | tf_op jit(solution)/shard_map/ppermute | solution.py:20
  257.5 8.5 %collective-permute-start.36 = (f32[1,512,128]{2,1,0:T(8,128)S(1)}, f32[1,512,128]{2,1,0:T(8,128)S(1)}, u32[]{:S(2)}, u32[]{:S(2)}) collective-permute-start(f32[1,512,128]{2,1,0:T(8,128)S(1)} %get-tuple-element.114), channel_id=1, source_target_pairs={{1,0},{2,1},{3,2},{5,4},{6,5},{7,6},{9,8},{10,9},{11,10},{13,12},{... | collective-permute-start | bytes 786440 | tf_op jit(solution)/shard_map/ppermute | solution.py:20
  268.4 8.5 %collective-permute-start.38 = (f32[1,512,128]{2,1,0:T(8,128)S(1)}, f32[1,512,128]{2,1,0:T(8,128)S(1)}, u32[]{:S(2)}, u32[]{:S(2)}) collective-permute-start(f32[1,512,128]{2,1,0:T(8,128)S(1)} %get-tuple-element.112), channel_id=1, source_target_pairs={{1,0},{2,1},{3,2},{5,4},{6,5},{7,6},{9,8},{10,9},{11,10},{13,12},{... | collective-permute-start | bytes 786440 | tf_op jit(solution)/shard_map/ppermute | solution.py:20
  279.2 8.5 %collective-permute-start.40 = (f32[1,512,128]{2,1,0:T(8,128)S(1)}, f32[1,512,128]{2,1,0:T(8,128)S(1)}, u32[]{:S(2)}, u32[]{:S(2)}) collective-permute-start(f32[1,512,128]{2,1,0:T(8,128)S(1)} %get-tuple-element.110), channel_id=1, source_target_pairs={{1,0},{2,1},{3,2},{5,4},{6,5},{7,6},{9,8},{10,9},{11,10},{13,12},{... | collective-permute-start | bytes 786440 | tf_op jit(solution)/shard_map/ppermute | solution.py:20
  290.0 8.9 %collective-permute-start.42 = (f32[1,512,128]{2,1,0:T(8,128)S(1)}, f32[1,512,128]{2,1,0:T(8,128)S(1)}, u32[]{:S(2)}, u32[]{:S(2)}) collective-permute-start(f32[1,512,128]{2,1,0:T(8,128)S(1)} %get-tuple-element.108), channel_id=1, source_target_pairs={{1,0},{2,1},{3,2},{5,4},{6,5},{7,6},{9,8},{10,9},{11,10},{13,12},{... | collective-permute-start | bytes 786440 | tf_op jit(solution)/shard_map/ppermute | solution.py:20
  300.8 8.5 %collective-permute-start.44 = (f32[1,512,128]{2,1,0:T(8,128)S(1)}, f32[1,512,128]{2,1,0:T(8,128)S(1)}, u32[]{:S(2)}, u32[]{:S(2)}) collective-permute-start(f32[1,512,128]{2,1,0:T(8,128)S(1)} %get-tuple-element.106), channel_id=1, source_target_pairs={{1,0},{2,1},{3,2},{5,4},{6,5},{7,6},{9,8},{10,9},{11,10},{13,12},{... | collective-permute-start | bytes 786440 | tf_op jit(solution)/shard_map/ppermute | solution.py:20
  311.6 8.5 %collective-permute-start.46 = (f32[1,512,128]{2,1,0:T(8,128)S(1)}, f32[1,512,128]{2,1,0:T(8,128)S(1)}, u32[]{:S(2)}, u32[]{:S(2)}) collective-permute-start(f32[1,512,128]{2,1,0:T(8,128)S(1)} %get-tuple-element.104), channel_id=1, source_target_pairs={{1,0},{2,1},{3,2},{5,4},{6,5},{7,6},{9,8},{10,9},{11,10},{13,12},{... | collective-permute-start | bytes 786440 | tf_op jit(solution)/shard_map/ppermute | solution.py:20
  322.7 8.5 %collective-permute-start.48 = (f32[1,512,128]{2,1,0:T(8,128)S(1)}, f32[1,512,128]{2,1,0:T(8,128)S(1)}, u32[]{:S(2)}, u32[]{:S(2)}) collective-permute-start(f32[1,512,128]{2,1,0:T(8,128)S(1)} %get-tuple-element.102), channel_id=1, source_target_pairs={{1,0},{2,1},{3,2},{5,4},{6,5},{7,6},{9,8},{10,9},{11,10},{13,12},{... | collective-permute-start | bytes 786440 | tf_op jit(solution)/shard_map/ppermute | solution.py:20
  333.5 8.5 %collective-permute-start.50 = (f32[1,512,128]{2,1,0:T(8,128)S(1)}, f32[1,512,128]{2,1,0:T(8,128)S(1)}, u32[]{:S(2)}, u32[]{:S(2)}) collective-permute-start(f32[1,512,128]{2,1,0:T(8,128)S(1)} %get-tuple-element.100), channel_id=1, source_target_pairs={{1,0},{2,1},{3,2},{5,4},{6,5},{7,6},{9,8},{10,9},{11,10},{13,12},{... | collective-permute-start | bytes 786440 | tf_op jit(solution)/shard_map/ppermute | solution.py:20
  344.3 8.5 %collective-permute-start.52 = (f32[1,512,128]{2,1,0:T(8,128)S(1)}, f32[1,512,128]{2,1,0:T(8,128)S(1)}, u32[]{:S(2)}, u32[]{:S(2)}) collective-permute-start(f32[1,512,128]{2,1,0:T(8,128)S(1)} %get-tuple-element.98), channel_id=1, source_target_pairs={{1,0},{2,1},{3,2},{5,4},{6,5},{7,6},{9,8},{10,9},{11,10},{13,12},{... | collective-permute-start | bytes 786440 | tf_op jit(solution)/shard_map/ppermute | solution.py:20
  355.1 8.5 %collective-permute-start.54 = (f32[1,512,128]{2,1,0:T(8,128)S(1)}, f32[1,512,128]{2,1,0:T(8,128)S(1)}, u32[]{:S(2)}, u32[]{:S(2)}) collective-permute-start(f32[1,512,128]{2,1,0:T(8,128)S(1)} %get-tuple-element.96), channel_id=1, source_target_pairs={{1,0},{2,1},{3,2},{5,4},{6,5},{7,6},{9,8},{10,9},{11,10},{13,12},{... | collective-permute-start | bytes 786440 | tf_op jit(solution)/shard_map/ppermute | solution.py:20
  365.9 8.5 %collective-permute-start.56 = (f32[1,512,128]{2,1,0:T(8,128)S(1)}, f32[1,512,128]{2,1,0:T(8,128)S(1)}, u32[]{:S(2)}, u32[]{:S(2)}) collective-permute-start(f32[1,512,128]{2,1,0:T(8,128)S(1)} %get-tuple-element.94), channel_id=1, source_target_pairs={{1,0},{2,1},{3,2},{5,4},{6,5},{7,6},{9,8},{10,9},{11,10},{13,12},{... | collective-permute-start | bytes 786440 | tf_op jit(solution)/shard_map/ppermute | solution.py:20
  376.7 8.7 %collective-permute-start.58 = (f32[1,512,128]{2,1,0:T(8,128)S(1)}, f32[1,512,128]{2,1,0:T(8,128)S(1)}, u32[]{:S(2)}, u32[]{:S(2)}) collective-permute-start(f32[1,512,128]{2,1,0:T(8,128)S(1)} %get-tuple-element.92), channel_id=1, source_target_pairs={{1,0},{2,1},{3,2},{5,4},{6,5},{7,6},{9,8},{10,9},{11,10},{13,12},{... | collective-permute-start | bytes 786440 | tf_op jit(solution)/shard_map/ppermute | solution.py:20
  387.8 8.5 %collective-permute-start.60 = (f32[1,512,128]{2,1,0:T(8,128)S(1)}, f32[1,512,128]{2,1,0:T(8,128)S(1)}, u32[]{:S(2)}, u32[]{:S(2)}) collective-permute-start(f32[1,512,128]{2,1,0:T(8,128)S(1)} %get-tuple-element.90), channel_id=1, source_target_pairs={{1,0},{2,1},{3,2},{5,4},{6,5},{7,6},{9,8},{10,9},{11,10},{13,12},{... | collective-permute-start | bytes 786440 | tf_op jit(solution)/shard_map/ppermute | solution.py:20
  398.6 8.5 %collective-permute-start.62 = (f32[1,512,128]{2,1,0:T(8,128)S(1)}, f32[1,512,128]{2,1,0:T(8,128)S(1)}, u32[]{:S(2)}, u32[]{:S(2)}) collective-permute-start(f32[1,512,128]{2,1,0:T(8,128)S(1)} %get-tuple-element.88), channel_id=1, source_target_pairs={{1,0},{2,1},{3,2},{5,4},{6,5},{7,6},{9,8},{10,9},{11,10},{13,12},{... | collective-permute-start | bytes 786440 | tf_op jit(solution)/shard_map/ppermute | solution.py:20
  409.4 8.5 %collective-permute-start.64 = (f32[1,512,128]{2,1,0:T(8,128)S(1)}, f32[1,512,128]{2,1,0:T(8,128)S(1)}, u32[]{:S(2)}, u32[]{:S(2)}) collective-permute-start(f32[1,512,128]{2,1,0:T(8,128)S(1)} %get-tuple-element.86), channel_id=1, source_target_pairs={{1,0},{2,1},{3,2},{5,4},{6,5},{7,6},{9,8},{10,9},{11,10},{13,12},{... | collective-permute-start | bytes 786440 | tf_op jit(solution)/shard_map/ppermute | solution.py:20
  420.2 8.5 %collective-permute-start.66 = (f32[1,512,128]{2,1,0:T(8,128)S(1)}, f32[1,512,128]{2,1,0:T(8,128)S(1)}, u32[]{:S(2)}, u32[]{:S(2)}) collective-permute-start(f32[1,512,128]{2,1,0:T(8,128)S(1)} %get-tuple-element.84), channel_id=1, source_target_pairs={{1,0},{2,1},{3,2},{5,4},{6,5},{7,6},{9,8},{10,9},{11,10},{13,12},{... | collective-permute-start | bytes 786440 | tf_op jit(solution)/shard_map/ppermute | solution.py:20
  431.0 8.5 %collective-permute-start.68 = (f32[1,512,128]{2,1,0:T(8,128)S(1)}, f32[1,512,128]{2,1,0:T(8,128)S(1)}, u32[]{:S(2)}, u32[]{:S(2)}) collective-permute-start(f32[1,512,128]{2,1,0:T(8,128)S(1)} %get-tuple-element.82), channel_id=1, source_target_pairs={{1,0},{2,1},{3,2},{5,4},{6,5},{7,6},{9,8},{10,9},{11,10},{13,12},{... | collective-permute-start | bytes 786440 | tf_op jit(solution)/shard_map/ppermute | solution.py:20
  441.8 8.5 %collective-permute-start.70 = (f32[1,512,128]{2,1,0:T(8,128)S(1)}, f32[1,512,128]{2,1,0:T(8,128)S(1)}, u32[]{:S(2)}, u32[]{:S(2)}) collective-permute-start(f32[1,512,128]{2,1,0:T(8,128)S(1)} %get-tuple-element.80), channel_id=1, source_target_pairs={{1,0},{2,1},{3,2},{5,4},{6,5},{7,6},{9,8},{10,9},{11,10},{13,12},{... | collective-permute-start | bytes 786440 | tf_op jit(solution)/shard_map/ppermute | solution.py:20
  (32 other events, 526.3 us)
Sparse Core Ops, SparseCore 0:
  10.1 51.9 all-gather.1
  455.6 105.8 all-reduce.38
where the time goes:
time: 581 us; the launch traced here: 570 us
  starting transfers between devices  301 us (52%)
  waiting for transfers between devices  199 us (34%)
  other arithmetic  42.4 us (7%)
  between operations  16.7 us (3%)
  local copies, waits for them, and re-layouts  7.08 us (1%)
    ppermute x36, starting transfers between devices, padded_2(): before = lax.ppermute(last, axis, up)  254 us
    unnamed x3, waiting for transfers between devices  105 us
    all_gather x1, waiting for transfers between devices, body(): shard_rows = lax.all_gather(conductivity, 'mesh', axis=1, tiled=True)  54.2 us
    ppermute x36, starting transfers between devices, padded_2(): after = lax.ppermute(leading, axis, down)  46.6 us
    ppermute x36, waiting for transfers between devices, padded_2(): before = lax.ppermute(last, axis, up)  39.3 us
    concatenate x36, other arithmetic, padded_2(): x = jnp.concatenate([before, x, after], axis=dim)  22.2 us
    add x30, other arithmetic, chebyshev(): ratio_next * ratio_now * direct + 2.0 * ratio_next / half_width * remain  15.6 us
  transfers between devices with their start and end apart: 74, of which 38 were waited for; matrix products, arithmetic and copies ran while one was open for 0% of the time, Pallas kernels for 0%

commit v1 on v0

--- a/solution.py
+++ b/solution.py
@@ -7,6 +7,26 @@
 DEG = 6
 low_bound = 0.3
 high_bound = 15.0
+
+
+def deliver_patches(t0, k_dim):
+    t0 = jnp.moveaxis(t0, 0, k_dim)
+    passed = t0.shape
+    return t0.reshape(*passed[:k_dim], passed[k_dim] * passed[k_dim + 1], *passed[k_dim + 2 :])
+
+
+def modes_detail(xx, shard_axis):
+    block_now = xx[None]
+    n_peers_all = jax.lax.axis_size(shard_axis)
+    for u in range(n_peers_all.bit_length() - 1):
+        seen_now = 1 << u
+        value_now = jax.lax.ppermute(
+            block_now, shard_axis, [(pp, pp ^ seen_now) for pp in range(n_peers_all)]
+        )
+        z2 = jnp.stack([block_now, value_now])
+        upper = jax.lax.axis_index(shard_axis) >> u & 1
+        block_now = jnp.where(upper == 0, z2, z2[::-1]).reshape(-1, *xx.shape)
+    return block_now
 
 
 def padded_2(x, sides, width):
@@ -70,7 +90,7 @@
     tile_count = footprint.shape[1]
     cell_count = depth * block_y * across
     my_blocks = lax.dynamic_index_in_dim(footprint, my_index, 0, keepdims=False)
-    shard_rows = lax.all_gather(conductivity, "mesh", axis=1, tiled=True)
+    shard_rows = deliver_patches(modes_detail(conductivity, "mesh"), 1)
     row_count = shard_rows.shape[1]
     flat_rows = shard_rows[0].reshape(row_count, cell_count)
     chosen = (my_blocks[:, None] == jnp.arange(row_count, dtype=jnp.int32)[None, :]).astype(

time: 581 us -> 601 us (1.034)
  waiting for transfers between devices: 199 us -> 212 us
    ppermute x0 -> x3, waiting for transfers between devices: none -> 62.1 us  [modes_detail(): jax.lax.ppermute(block_now, shard_axis, [(pp, pp ^ seen_now) for pp in ra...]
    all_gather x1 -> x0, waiting for transfers between devices: 54.2 us -> none  [body(): shard_rows = lax.all_gather(conductivity, 'mesh', axis=1, tiled=True)]
    ppermute x0 -> x3, starting transfers between devices: none -> 7.48 us  [modes_detail(): jax.lax.ppermute(block_now, shard_axis, [(pp, pp ^ seen_now) for pp in ra...]
    unnamed x3 -> x2, waiting for transfers between devices: 105 us -> 107 us
  transfers between devices with their start and end apart: 74 -> 76, of which waited for: 38 -> 40; matrix products, arithmetic and copies ran while one was open for 0% -> 0% of each run, Pallas kernels for 0% -> 0%
where the time goes in v1:
time: 601 us; the launch traced here: 591 us
  starting transfers between devices  307 us (51%)
  waiting for transfers between devices  212 us (35%)
  other arithmetic  44.1 us (7%)
  between operations  16.7 us (3%)
  local copies, waits for them, and re-layouts  7.37 us (1%)
    ppermute x36, starting transfers between devices, padded_2(): before = lax.ppermute(last, axis, up)  252 us
    unnamed x2, waiting for transfers between devices  107 us
    ppermute x3, waiting for transfers between devices, modes_detail(): jax.lax.ppermute(block_now, shard_axis, [(pp, pp ^ seen_now) for pp in ra...  62.1 us
    ppermute x36, starting transfers between devices, padded_2(): after = lax.ppermute(leading, axis, down)  46.6 us
    ppermute x36, waiting for transfers between devices, padded_2(): before = lax.ppermute(last, axis, up)  38.2 us
    concatenate x36, other arithmetic, padded_2(): x = jnp.concatenate([before, x, after], axis=dim)  22.2 us
    add x30, other arithmetic, chebyshev(): ratio_next * ratio_now * direct + 2.0 * ratio_next / half_width * remain  15.6 us
  transfers between devices with their start and end apart: 76, of which 40 were waited for; matrix products, arithmetic and copies ran while one was open for 0% of the time, Pallas kernels for 0%

profile of v1, /device:TPU:0, one launch (start us, length us, event | category | flops | bytes accessed | tf_op | source)
XLA Modules:
  0.0 591.1 jit_solution(5356512839081752207)
XLA Ops:
  7.2 3.0 collective-permute-start
  10.2 6.5 %collective-permute-done = f32[1,1,4,2,64,128]{5,4,3,2,1,0:T(8,128)S(1)} collective-permute-done((f32[1,1,4,2,64,128]{5,4,3,2,1,0:T(8,128)}, f32[1,1,4,2,64,128]{5,4,3,2,1,0:T(8,128)S(1)}, u32[]{:S(2)}, u32[]{:S(2)}) %collective-permute-start) | collective-permute-done | bytes 262176 | tf_op jit(solution)/shard_map/ppermute | solution.py:23
  17.9 1.9 collective-permute-start.1
  19.8 11.3 %collective-permute-done.1 = f32[2,1,4,2,64,128]{5,4,3,2,0,1:T(8,128)S(1)} collective-permute-done((f32[2,1,4,2,64,128]{5,4,3,2,0,1:T(8,128)S(1)}, f32[2,1,4,2,64,128]{5,4,3,2,0,1:T(8,128)S(1)}, u32[]{:S(2)}, u32[]{:S(2)}) %collective-permute-start.1) | collective-permute-done | bytes 524320 | tf_op jit(solution)/shard_map/ppermute | solution.py:23
  31.3 2.6 collective-permute-start.2
  33.9 44.3 %collective-permute-done.2 = f32[4,1,4,2,64,128]{5,4,3,2,0,1:T(8,128)S(1)} collective-permute-done((f32[4,1,4,2,64,128]{5,4,3,2,0,1:T(8,128)S(1)}, f32[4,1,4,2,64,128]{5,4,3,2,0,1:T(8,128)S(1)}, u32[]{:S(2)}, u32[]{:S(2)}) %collective-permute-start.2) | collective-permute-done | bytes 1048608 | tf_op jit(solution)/shard_map/ppermute | solution.py:23
  78.5 1.5 reshape_squeeze_reshape_transpose_reshape.3
  80.0 2.0 copy.13
  82.0 2.0 fusion.5
  85.6 3.0 collective-permute-start.4
  92.3 5.5 collective-permute-start.6
  101.3 7.2 %collective-permute-start.8 = (f32[1,512,128]{2,1,0:T(8,128)S(1)}, f32[1,512,128]{2,1,0:T(8,128)S(1)}, u32[]{:S(2)}, u32[]{:S(2)}) collective-permute-start(f32[1,512,128]{2,1,0:T(8,128)S(1)} %get-tuple-element.145), channel_id=1, source_target_pairs={{0,1},{1,2},{2,3},{4,5},{5,6},{6,7},{8,9},{9,10},{10,11},{12,13},{... | collective-permute-start | bytes 786440 | tf_op jit(solution)/shard_map/ppermute | solution.py:39
  110.9 6.6 %collective-permute-start.10 = (f32[1,512,128]{2,1,0:T(8,128)S(1)}, f32[1,512,128]{2,1,0:T(8,128)S(1)}, u32[]{:S(2)}, u32[]{:S(2)}) collective-permute-start(f32[1,512,128]{2,1,0:T(8,128)S(1)} %get-tuple-element.143), channel_id=1, source_target_pairs={{0,1},{1,2},{2,3},{4,5},{5,6},{6,7},{8,9},{9,10},{10,11},{12,13},{... | collective-permute-start | bytes 786440 | tf_op jit(solution)/shard_map/ppermute | solution.py:39
  118.7 4.1 collective-permute-done.9
  125.3 7.3 %collective-permute-start.12 = (f32[1,512,128]{2,1,0:T(8,128)S(1)}, f32[1,512,128]{2,1,0:T(8,128)S(1)}, u32[]{:S(2)}, u32[]{:S(2)}) collective-permute-start(f32[1,512,128]{2,1,0:T(8,128)S(1)} %get-tuple-element.141), channel_id=1, source_target_pairs={{0,1},{1,2},{2,3},{4,5},{5,6},{6,7},{8,9},{9,10},{10,11},{12,13},{... | collective-permute-start | bytes 786440 | tf_op jit(solution)/shard_map/ppermute | solution.py:39
  136.3 6.6 %collective-permute-start.14 = (f32[1,512,128]{2,1,0:T(8,128)S(1)}, f32[1,512,128]{2,1,0:T(8,128)S(1)}, u32[]{:S(2)}, u32[]{:S(2)}) collective-permute-start(f32[1,512,128]{2,1,0:T(8,128)S(1)} %get-tuple-element.139), channel_id=1, source_target_pairs={{0,1},{1,2},{2,3},{4,5},{5,6},{6,7},{8,9},{9,10},{10,11},{12,13},{... | collective-permute-start | bytes 786440 | tf_op jit(solution)/shard_map/ppermute | solution.py:39
  146.5 7.2 %collective-permute-start.16 = (f32[1,512,128]{2,1,0:T(8,128)S(1)}, f32[1,512,128]{2,1,0:T(8,128)S(1)}, u32[]{:S(2)}, u32[]{:S(2)}) collective-permute-start(f32[1,512,128]{2,1,0:T(8,128)S(1)} %get-tuple-element.137), channel_id=1, source_target_pairs={{0,1},{1,2},{2,3},{4,5},{5,6},{6,7},{8,9},{9,10},{10,11},{12,13},{... | collective-permute-start | bytes 786440 | tf_op jit(solution)/shard_map/ppermute | solution.py:39
  157.3 7.2 %collective-permute-start.18 = (f32[1,512,128]{2,1,0:T(8,128)S(1)}, f32[1,512,128]{2,1,0:T(8,128)S(1)}, u32[]{:S(2)}, u32[]{:S(2)}) collective-permute-start(f32[1,512,128]{2,1,0:T(8,128)S(1)} %get-tuple-element.135), channel_id=1, source_target_pairs={{0,1},{1,2},{2,3},{4,5},{5,6},{6,7},{8,9},{9,10},{10,11},{12,13},{... | collective-permute-start | bytes 786440 | tf_op jit(solution)/shard_map/ppermute | solution.py:39
  168.1 7.2 %collective-permute-start.20 = (f32[1,512,128]{2,1,0:T(8,128)S(1)}, f32[1,512,128]{2,1,0:T(8,128)S(1)}, u32[]{:S(2)}, u32[]{:S(2)}) collective-permute-start(f32[1,512,128]{2,1,0:T(8,128)S(1)} %get-tuple-element.133), channel_id=1, source_target_pairs={{0,1},{1,2},{2,3},{4,5},{5,6},{6,7},{8,9},{9,10},{10,11},{12,13},{... | collective-permute-start | bytes 786440 | tf_op jit(solution)/shard_map/ppermute | solution.py:39
  179.0 7.2 %collective-permute-start.22 = (f32[1,512,128]{2,1,0:T(8,128)S(1)}, f32[1,512,128]{2,1,0:T(8,128)S(1)}, u32[]{:S(2)}, u32[]{:S(2)}) collective-permute-start(f32[1,512,128]{2,1,0:T(8,128)S(1)} %get-tuple-element.131), channel_id=1, source_target_pairs={{0,1},{1,2},{2,3},{4,5},{5,6},{6,7},{8,9},{9,10},{10,11},{12,13},{... | collective-permute-start | bytes 786440 | tf_op jit(solution)/shard_map/ppermute | solution.py:39
  189.8 7.2 %collective-permute-start.24 = (f32[1,512,128]{2,1,0:T(8,128)S(1)}, f32[1,512,128]{2,1,0:T(8,128)S(1)}, u32[]{:S(2)}, u32[]{:S(2)}) collective-permute-start(f32[1,512,128]{2,1,0:T(8,128)S(1)} %get-tuple-element.129), channel_id=1, source_target_pairs={{0,1},{1,2},{2,3},{4,5},{5,6},{6,7},{8,9},{9,10},{10,11},{12,13},{... | collective-permute-start | bytes 786440 | tf_op jit(solution)/shard_map/ppermute | solution.py:39
  200.6 7.2 %collective-permute-start.26 = (f32[1,512,128]{2,1,0:T(8,128)S(1)}, f32[1,512,128]{2,1,0:T(8,128)S(1)}, u32[]{:S(2)}, u32[]{:S(2)}) collective-permute-start(f32[1,512,128]{2,1,0:T(8,128)S(1)} %get-tuple-element.127), channel_id=1, source_target_pairs={{0,1},{1,2},{2,3},{4,5},{5,6},{6,7},{8,9},{9,10},{10,11},{12,13},{... | collective-permute-start | bytes 786440 | tf_op jit(solution)/shard_map/ppermute | solution.py:39
  211.6 7.2 %collective-permute-start.28 = (f32[1,512,128]{2,1,0:T(8,128)S(1)}, f32[1,512,128]{2,1,0:T(8,128)S(1)}, u32[]{:S(2)}, u32[]{:S(2)}) collective-permute-start(f32[1,512,128]{2,1,0:T(8,128)S(1)} %get-tuple-element.125), channel_id=1, source_target_pairs={{0,1},{1,2},{2,3},{4,5},{5,6},{6,7},{8,9},{9,10},{10,11},{12,13},{... | collective-permute-start | bytes 786440 | tf_op jit(solution)/shard_map/ppermute | solution.py:39
  222.4 7.4 %collective-permute-start.30 = (f32[1,512,128]{2,1,0:T(8,128)S(1)}, f32[1,512,128]{2,1,0:T(8,128)S(1)}, u32[]{:S(2)}, u32[]{:S(2)}) collective-permute-start(f32[1,512,128]{2,1,0:T(8,128)S(1)} %get-tuple-element.123), channel_id=1, source_target_pairs={{0,1},{1,2},{2,3},{4,5},{5,6},{6,7},{8,9},{9,10},{10,11},{12,13},{... | collective-permute-start | bytes 786440 | tf_op jit(solution)/shard_map/ppermute | solution.py:39
  233.3 7.2 %collective-permute-start.32 = (f32[1,512,128]{2,1,0:T(8,128)S(1)}, f32[1,512,128]{2,1,0:T(8,128)S(1)}, u32[]{:S(2)}, u32[]{:S(2)}) collective-permute-start(f32[1,512,128]{2,1,0:T(8,128)S(1)} %get-tuple-element.121), channel_id=1, source_target_pairs={{0,1},{1,2},{2,3},{4,5},{5,6},{6,7},{8,9},{9,10},{10,11},{12,13},{... | collective-permute-start | bytes 786440 | tf_op jit(solution)/shard_map/ppermute | solution.py:39
  244.1 7.2 %collective-permute-start.34 = (f32[1,512,128]{2,1,0:T(8,128)S(1)}, f32[1,512,128]{2,1,0:T(8,128)S(1)}, u32[]{:S(2)}, u32[]{:S(2)}) collective-permute-start(f32[1,512,128]{2,1,0:T(8,128)S(1)} %get-tuple-element.119), channel_id=1, source_target_pairs={{0,1},{1,2},{2,3},{4,5},{5,6},{6,7},{8,9},{9,10},{10,11},{12,13},{... | collective-permute-start | bytes 786440 | tf_op jit(solution)/shard_map/ppermute | solution.py:39
  254.9 7.2 %collective-permute-start.36 = (f32[1,512,128]{2,1,0:T(8,128)S(1)}, f32[1,512,128]{2,1,0:T(8,128)S(1)}, u32[]{:S(2)}, u32[]{:S(2)}) collective-permute-start(f32[1,512,128]{2,1,0:T(8,128)S(1)} %get-tuple-element.117), channel_id=1, source_target_pairs={{0,1},{1,2},{2,3},{4,5},{5,6},{6,7},{8,9},{9,10},{10,11},{12,13},{... | collective-permute-start | bytes 786440 | tf_op jit(solution)/shard_map/ppermute | solution.py:39
  265.8 7.2 %collective-permute-start.38 = (f32[1,512,128]{2,1,0:T(8,128)S(1)}, f32[1,512,128]{2,1,0:T(8,128)S(1)}, u32[]{:S(2)}, u32[]{:S(2)}) collective-permute-start(f32[1,512,128]{2,1,0:T(8,128)S(1)} %get-tuple-element.115), channel_id=1, source_target_pairs={{0,1},{1,2},{2,3},{4,5},{5,6},{6,7},{8,9},{9,10},{10,11},{12,13},{... | collective-permute-start | bytes 786440 | tf_op jit(solution)/shard_map/ppermute | solution.py:39
  276.9 7.2 %collective-permute-start.40 = (f32[1,512,128]{2,1,0:T(8,128)S(1)}, f32[1,512,128]{2,1,0:T(8,128)S(1)}, u32[]{:S(2)}, u32[]{:S(2)}) collective-permute-start(f32[1,512,128]{2,1,0:T(8,128)S(1)} %get-tuple-element.113), channel_id=1, source_target_pairs={{0,1},{1,2},{2,3},{4,5},{5,6},{6,7},{8,9},{9,10},{10,11},{12,13},{... | collective-permute-start | bytes 786440 | tf_op jit(solution)/shard_map/ppermute | solution.py:39
  287.7 7.2 %collective-permute-start.42 = (f32[1,512,128]{2,1,0:T(8,128)S(1)}, f32[1,512,128]{2,1,0:T(8,128)S(1)}, u32[]{:S(2)}, u32[]{:S(2)}) collective-permute-start(f32[1,512,128]{2,1,0:T(8,128)S(1)} %get-tuple-element.111), channel_id=1, source_target_pairs={{0,1},{1,2},{2,3},{4,5},{5,6},{6,7},{8,9},{9,10},{10,11},{12,13},{... | collective-permute-start | bytes 786440 | tf_op jit(solution)/shard_map/ppermute | solution.py:39
  298.5 7.2 %collective-permute-start.44 = (f32[1,512,128]{2,1,0:T(8,128)S(1)}, f32[1,512,128]{2,1,0:T(8,128)S(1)}, u32[]{:S(2)}, u32[]{:S(2)}) collective-permute-start(f32[1,512,128]{2,1,0:T(8,128)S(1)} %get-tuple-element.109), channel_id=1, source_target_pairs={{0,1},{1,2},{2,3},{4,5},{5,6},{6,7},{8,9},{9,10},{10,11},{12,13},{... | collective-permute-start | bytes 786440 | tf_op jit(solution)/shard_map/ppermute | solution.py:39
  309.3 7.6 %collective-permute-start.46 = (f32[1,512,128]{2,1,0:T(8,128)S(1)}, f32[1,512,128]{2,1,0:T(8,128)S(1)}, u32[]{:S(2)}, u32[]{:S(2)}) collective-permute-start(f32[1,512,128]{2,1,0:T(8,128)S(1)} %get-tuple-element.107), channel_id=1, source_target_pairs={{0,1},{1,2},{2,3},{4,5},{5,6},{6,7},{8,9},{9,10},{10,11},{12,13},{... | collective-permute-start | bytes 786440 | tf_op jit(solution)/shard_map/ppermute | solution.py:39
  320.1 7.2 %collective-permute-start.48 = (f32[1,512,128]{2,1,0:T(8,128)S(1)}, f32[1,512,128]{2,1,0:T(8,128)S(1)}, u32[]{:S(2)}, u32[]{:S(2)}) collective-permute-start(f32[1,512,128]{2,1,0:T(8,128)S(1)} %get-tuple-element.105), channel_id=1, source_target_pairs={{0,1},{1,2},{2,3},{4,5},{5,6},{6,7},{8,9},{9,10},{10,11},{12,13},{... | collective-permute-start | bytes 786440 | tf_op jit(solution)/shard_map/ppermute | solution.py:39
  330.9 7.2 %collective-permute-start.50 = (f32[1,512,128]{2,1,0:T(8,128)S(1)}, f32[1,512,128]{2,1,0:T(8,128)S(1)}, u32[]{:S(2)}, u32[]{:S(2)}) collective-permute-start(f32[1,512,128]{2,1,0:T(8,128)S(1)} %get-tuple-element.103), channel_id=1, source_target_pairs={{0,1},{1,2},{2,3},{4,5},{5,6},{6,7},{8,9},{9,10},{10,11},{12,13},{... | collective-permute-start | bytes 786440 | tf_op jit(solution)/shard_map/ppermute | solution.py:39
  342.0 7.2 %collective-permute-start.52 = (f32[1,512,128]{2,1,0:T(8,128)S(1)}, f32[1,512,128]{2,1,0:T(8,128)S(1)}, u32[]{:S(2)}, u32[]{:S(2)}) collective-permute-start(f32[1,512,128]{2,1,0:T(8,128)S(1)} %get-tuple-element.101), channel_id=1, source_target_pairs={{0,1},{1,2},{2,3},{4,5},{5,6},{6,7},{8,9},{9,10},{10,11},{12,13},{... | collective-permute-start | bytes 786440 | tf_op jit(solution)/shard_map/ppermute | solution.py:39
  352.8 7.2 %collective-permute-start.54 = (f32[1,512,128]{2,1,0:T(8,128)S(1)}, f32[1,512,128]{2,1,0:T(8,128)S(1)}, u32[]{:S(2)}, u32[]{:S(2)}) collective-permute-start(f32[1,512,128]{2,1,0:T(8,128)S(1)} %get-tuple-element.99), channel_id=1, source_target_pairs={{0,1},{1,2},{2,3},{4,5},{5,6},{6,7},{8,9},{9,10},{10,11},{12,13},{... | collective-permute-start | bytes 786440 | tf_op jit(solution)/shard_map/ppermute | solution.py:39
  363.6 7.2 %collective-permute-start.56 = (f32[1,512,128]{2,1,0:T(8,128)S(1)}, f32[1,512,128]{2,1,0:T(8,128)S(1)}, u32[]{:S(2)}, u32[]{:S(2)}) collective-permute-start(f32[1,512,128]{2,1,0:T(8,128)S(1)} %get-tuple-element.97), channel_id=1, source_target_pairs={{0,1},{1,2},{2,3},{4,5},{5,6},{6,7},{8,9},{9,10},{10,11},{12,13},{... | collective-permute-start | bytes 786440 | tf_op jit(solution)/shard_map/ppermute | solution.py:39
  374.5 7.2 %collective-permute-start.58 = (f32[1,512,128]{2,1,0:T(8,128)S(1)}, f32[1,512,128]{2,1,0:T(8,128)S(1)}, u32[]{:S(2)}, u32[]{:S(2)}) collective-permute-start(f32[1,512,128]{2,1,0:T(8,128)S(1)} %get-tuple-element.95), channel_id=1, source_target_pairs={{0,1},{1,2},{2,3},{4,5},{5,6},{6,7},{8,9},{9,10},{10,11},{12,13},{... | collective-permute-start | bytes 786440 | tf_op jit(solution)/shard_map/ppermute | solution.py:39
  385.3 7.2 %collective-permute-start.60 = (f32[1,512,128]{2,1,0:T(8,128)S(1)}, f32[1,512,128]{2,1,0:T(8,128)S(1)}, u32[]{:S(2)}, u32[]{:S(2)}) collective-permute-start(f32[1,512,128]{2,1,0:T(8,128)S(1)} %get-tuple-element.93), channel_id=1, source_target_pairs={{0,1},{1,2},{2,3},{4,5},{5,6},{6,7},{8,9},{9,10},{10,11},{12,13},{... | collective-permute-start | bytes 786440 | tf_op jit(solution)/shard_map/ppermute | solution.py:39
  396.1 7.4 %collective-permute-start.62 = (f32[1,512,128]{2,1,0:T(8,128)S(1)}, f32[1,512,128]{2,1,0:T(8,128)S(1)}, u32[]{:S(2)}, u32[]{:S(2)}) collective-permute-start(f32[1,512,128]{2,1,0:T(8,128)S(1)} %get-tuple-element.91), channel_id=1, source_target_pairs={{0,1},{1,2},{2,3},{4,5},{5,6},{6,7},{8,9},{9,10},{10,11},{12,13},{... | collective-permute-start | bytes 786440 | tf_op jit(solution)/shard_map/ppermute | solution.py:39
  407.1 7.2 %collective-permute-start.64 = (f32[1,512,128]{2,1,0:T(8,128)S(1)}, f32[1,512,128]{2,1,0:T(8,128)S(1)}, u32[]{:S(2)}, u32[]{:S(2)}) collective-permute-start(f32[1,512,128]{2,1,0:T(8,128)S(1)} %get-tuple-element.89), channel_id=1, source_target_pairs={{0,1},{1,2},{2,3},{4,5},{5,6},{6,7},{8,9},{9,10},{10,11},{12,13},{... | collective-permute-start | bytes 786440 | tf_op jit(solution)/shard_map/ppermute | solution.py:39
  417.9 7.2 %collective-permute-start.66 = (f32[1,512,128]{2,1,0:T(8,128)S(1)}, f32[1,512,128]{2,1,0:T(8,128)S(1)}, u32[]{:S(2)}, u32[]{:S(2)}) collective-permute-start(f32[1,512,128]{2,1,0:T(8,128)S(1)} %get-tuple-element.87), channel_id=1, source_target_pairs={{0,1},{1,2},{2,3},{4,5},{5,6},{6,7},{8,9},{9,10},{10,11},{12,13},{... | collective-permute-start | bytes 786440 | tf_op jit(solution)/shard_map/ppermute | solution.py:39
  428.7 7.2 %collective-permute-start.68 = (f32[1,512,128]{2,1,0:T(8,128)S(1)}, f32[1,512,128]{2,1,0:T(8,128)S(1)}, u32[]{:S(2)}, u32[]{:S(2)}) collective-permute-start(f32[1,512,128]{2,1,0:T(8,128)S(1)} %get-tuple-element.85), channel_id=1, source_target_pairs={{0,1},{1,2},{2,3},{4,5},{5,6},{6,7},{8,9},{9,10},{10,11},{12,13},{... | collective-permute-start | bytes 786440 | tf_op jit(solution)/shard_map/ppermute | solution.py:39
  439.5 7.2 %collective-permute-start.70 = (f32[1,512,128]{2,1,0:T(8,128)S(1)}, f32[1,512,128]{2,1,0:T(8,128)S(1)}, u32[]{:S(2)}, u32[]{:S(2)}) collective-permute-start(f32[1,512,128]{2,1,0:T(8,128)S(1)} %get-tuple-element.83), channel_id=1, source_target_pairs={{0,1},{1,2},{2,3},{4,5},{5,6},{6,7},{8,9},{9,10},{10,11},{12,13},{... | collective-permute-start | bytes 786440 | tf_op jit(solution)/shard_map/ppermute | solution.py:39
  450.4 7.2 %collective-permute-start.72 = (f32[1,512,128]{2,1,0:T(8,128)S(1)}, f32[1,512,128]{2,1,0:T(8,128)S(1)}, u32[]{:S(2)}, u32[]{:S(2)}) collective-permute-start(f32[1,512,128]{2,1,0:T(8,128)S(1)} %get-tuple-element.81), channel_id=1, source_target_pairs={{0,1},{1,2},{2,3},{4,5},{5,6},{6,7},{8,9},{9,10},{10,11},{12,13},{... | collective-permute-start | bytes 786440 | tf_op jit(solution)/shard_map/ppermute | solution.py:39
  461.2 7.2 %collective-permute-start.74 = (f32[1,512,128]{2,1,0:T(8,128)S(1)}, f32[1,512,128]{2,1,0:T(8,128)S(1)}, u32[]{:S(2)}, u32[]{:S(2)}) collective-permute-start(f32[1,512,128]{2,1,0:T(8,128)S(1)} %get-tuple-element.79), channel_id=1, source_target_pairs={{0,1},{1,2},{2,3},{4,5},{5,6},{6,7},{8,9},{9,10},{10,11},{12,13},{... | collective-permute-start | bytes 786440 | tf_op jit(solution)/shard_map/ppermute | solution.py:39
  471.1 2.4 fusion.8
  474.8 107.5 %all-reduce.39.cloned.1.call-done = f32[32,16384]{1,0:T(8,128)} async-done(((f32[32,16384]{1,0:T(8,128)}), f32[32,16384]{1,0:T(8,128)}) %all-reduce.39.cloned.1.call-update) | async-done | bytes 2097168
  (242 shorter events, 132.9 us)
Async XLA Ops:
  7.2 575.1 %all-reduce.39.cloned.1.call-start = ((), (), s32[]{:S(2)}) async-start(), calls=%async_computation | async-start | bytes 4194304
  7.2 9.5 %collective-permute-start = (f32[1,1,4,2,64,128]{5,4,3,2,1,0:T(8,128)}, f32[1,1,4,2,64,128]{5,4,3,2,1,0:T(8,128)S(1)}, u32[]{:S(2)}, u32[]{:S(2)}) collective-permute-start(f32[1,1,4,2,64,128]{5,4,3,2,1,0:T(8,128)} %bitcast.201), channel_id=1, source_target_pairs={{0,4},{4,0},{8,12},{12,8},{16,20},{20,16},{24,28},{28,24},{1,5},{5... | collective-permute-start | bytes 786440 | tf_op jit(solution)/shard_map/ppermute | solution.py:23
  17.9 13.2 %collective-permute-start.1 = (f32[2,1,4,2,64,128]{5,4,3,2,0,1:T(8,128)S(1)}, f32[2,1,4,2,64,128]{5,4,3,2,0,1:T(8,128)S(1)}, u32[]{:S(2)}, u32[]{:S(2)}) collective-permute-start(f32[2,1,4,2,64,128]{5,4,3,2,0,1:T(8,128)S(1)} %get-tuple-element.152), channel_id=1, source_target_pairs={{0,8},{4,12},{8,0},{12,4},{16,24},{20,28},{24,16},{28,20},{1,9},{5... | collective-permute-start | bytes 1572872 | tf_op jit(solution)/shard_map/ppermute | solution.py:23
  31.3 46.9 %collective-permute-start.2 = (f32[4,1,4,2,64,128]{5,4,3,2,0,1:T(8,128)S(1)}, f32[4,1,4,2,64,128]{5,4,3,2,0,1:T(8,128)S(1)}, u32[]{:S(2)}, u32[]{:S(2)}) collective-permute-start(f32[4,1,4,2,64,128]{5,4,3,2,0,1:T(8,128)S(1)} %bitcast.193), channel_id=1, source_target_pairs={{0,16},{4,20},{8,24},{12,28},{16,0},{20,4},{24,8},{28,12},{1,17},{... | collective-permute-start | bytes 3145736 | tf_op jit(solution)/shard_map/ppermute | solution.py:23
  100.0 8.5 %collective-permute-start.7 = (f32[1,512,128]{2,1,0:T(8,128)S(1)}, f32[1,512,128]{2,1,0:T(8,128)S(1)}, u32[]{:S(2)}, u32[]{:S(2)}) collective-permute-start(f32[1,512,128]{2,1,0:T(8,128)S(1)} %get-tuple-element.146), channel_id=1, source_target_pairs={{1,0},{2,1},{3,2},{5,4},{6,5},{7,6},{9,8},{10,9},{11,10},{13,12},{... | collective-permute-start | bytes 786440 | tf_op jit(solution)/shard_map/ppermute | solution.py:40
  101.3 8.3 %collective-permute-start.8 = (f32[1,512,128]{2,1,0:T(8,128)S(1)}, f32[1,512,128]{2,1,0:T(8,128)S(1)}, u32[]{:S(2)}, u32[]{:S(2)}) collective-permute-start(f32[1,512,128]{2,1,0:T(8,128)S(1)} %get-tuple-element.145), channel_id=1, source_target_pairs={{0,1},{1,2},{2,3},{4,5},{5,6},{6,7},{8,9},{9,10},{10,11},{12,13},{... | collective-permute-start | bytes 786440 | tf_op jit(solution)/shard_map/ppermute | solution.py:39
  124.0 8.6 %collective-permute-start.11 = (f32[1,512,128]{2,1,0:T(8,128)S(1)}, f32[1,512,128]{2,1,0:T(8,128)S(1)}, u32[]{:S(2)}, u32[]{:S(2)}) collective-permute-start(f32[1,512,128]{2,1,0:T(8,128)S(1)} %get-tuple-element.142), channel_id=1, source_target_pairs={{1,0},{2,1},{3,2},{5,4},{6,5},{7,6},{9,8},{10,9},{11,10},{13,12},{... | collective-permute-start | bytes 786440 | tf_op jit(solution)/shard_map/ppermute | solution.py:40
  125.3 8.4 %collective-permute-start.12 = (f32[1,512,128]{2,1,0:T(8,128)S(1)}, f32[1,512,128]{2,1,0:T(8,128)S(1)}, u32[]{:S(2)}, u32[]{:S(2)}) collective-permute-start(f32[1,512,128]{2,1,0:T(8,128)S(1)} %get-tuple-element.141), channel_id=1, source_target_pairs={{0,1},{1,2},{2,3},{4,5},{5,6},{6,7},{8,9},{9,10},{10,11},{12,13},{... | collective-permute-start | bytes 786440 | tf_op jit(solution)/shard_map/ppermute | solution.py:39
  145.2 8.5 %collective-permute-start.15 = (f32[1,512,128]{2,1,0:T(8,128)S(1)}, f32[1,512,128]{2,1,0:T(8,128)S(1)}, u32[]{:S(2)}, u32[]{:S(2)}) collective-permute-start(f32[1,512,128]{2,1,0:T(8,128)S(1)} %get-tuple-element.138), channel_id=1, source_target_pairs={{1,0},{2,1},{3,2},{5,4},{6,5},{7,6},{9,8},{10,9},{11,10},{13,12},{... | collective-permute-start | bytes 786440 | tf_op jit(solution)/shard_map/ppermute | solution.py:40
  146.5 8.3 %collective-permute-start.16 = (f32[1,512,128]{2,1,0:T(8,128)S(1)}, f32[1,512,128]{2,1,0:T(8,128)S(1)}, u32[]{:S(2)}, u32[]{:S(2)}) collective-permute-start(f32[1,512,128]{2,1,0:T(8,128)S(1)} %get-tuple-element.137), channel_id=1, source_target_pairs={{0,1},{1,2},{2,3},{4,5},{5,6},{6,7},{8,9},{9,10},{10,11},{12,13},{... | collective-permute-start | bytes 786440 | tf_op jit(solution)/shard_map/ppermute | solution.py:39
  156.0 8.5 %collective-permute-start.17 = (f32[1,512,128]{2,1,0:T(8,128)S(1)}, f32[1,512,128]{2,1,0:T(8,128)S(1)}, u32[]{:S(2)}, u32[]{:S(2)}) collective-permute-start(f32[1,512,128]{2,1,0:T(8,128)S(1)} %get-tuple-element.136), channel_id=1, source_target_pairs={{1,0},{2,1},{3,2},{5,4},{6,5},{7,6},{9,8},{10,9},{11,10},{13,12},{... | collective-permute-start | bytes 786440 | tf_op jit(solution)/shard_map/ppermute | solution.py:40
  157.3 8.3 %collective-permute-start.18 = (f32[1,512,128]{2,1,0:T(8,128)S(1)}, f32[1,512,128]{2,1,0:T(8,128)S(1)}, u32[]{:S(2)}, u32[]{:S(2)}) collective-permute-start(f32[1,512,128]{2,1,0:T(8,128)S(1)} %get-tuple-element.135), channel_id=1, source_target_pairs={{0,1},{1,2},{2,3},{4,5},{5,6},{6,7},{8,9},{9,10},{10,11},{12,13},{... | collective-permute-start | bytes 786440 | tf_op jit(solution)/shard_map/ppermute | solution.py:39
  166.8 8.5 %collective-permute-start.19 = (f32[1,512,128]{2,1,0:T(8,128)S(1)}, f32[1,512,128]{2,1,0:T(8,128)S(1)}, u32[]{:S(2)}, u32[]{:S(2)}) collective-permute-start(f32[1,512,128]{2,1,0:T(8,128)S(1)} %get-tuple-element.134), channel_id=1, source_target_pairs={{1,0},{2,1},{3,2},{5,4},{6,5},{7,6},{9,8},{10,9},{11,10},{13,12},{... | collective-permute-start | bytes 786440 | tf_op jit(solution)/shard_map/ppermute | solution.py:40
  168.1 8.3 %collective-permute-start.20 = (f32[1,512,128]{2,1,0:T(8,128)S(1)}, f32[1,512,128]{2,1,0:T(8,128)S(1)}, u32[]{:S(2)}, u32[]{:S(2)}) collective-permute-start(f32[1,512,128]{2,1,0:T(8,128)S(1)} %get-tuple-element.133), channel_id=1, source_target_pairs={{0,1},{1,2},{2,3},{4,5},{5,6},{6,7},{8,9},{9,10},{10,11},{12,13},{... | collective-permute-start | bytes 786440 | tf_op jit(solution)/shard_map/ppermute | solution.py:39
  177.7 8.5 %collective-permute-start.21 = (f32[1,512,128]{2,1,0:T(8,128)S(1)}, f32[1,512,128]{2,1,0:T(8,128)S(1)}, u32[]{:S(2)}, u32[]{:S(2)}) collective-permute-start(f32[1,512,128]{2,1,0:T(8,128)S(1)} %get-tuple-element.132), channel_id=1, source_target_pairs={{1,0},{2,1},{3,2},{5,4},{6,5},{7,6},{9,8},{10,9},{11,10},{13,12},{... | collective-permute-start | bytes 786440 | tf_op jit(solution)/shard_map/ppermute | solution.py:40
  179.0 8.3 %collective-permute-start.22 = (f32[1,512,128]{2,1,0:T(8,128)S(1)}, f32[1,512,128]{2,1,0:T(8,128)S(1)}, u32[]{:S(2)}, u32[]{:S(2)}) collective-permute-start(f32[1,512,128]{2,1,0:T(8,128)S(1)} %get-tuple-element.131), channel_id=1, source_target_pairs={{0,1},{1,2},{2,3},{4,5},{5,6},{6,7},{8,9},{9,10},{10,11},{12,13},{... | collective-permute-start | bytes 786440 | tf_op jit(solution)/shard_map/ppermute | solution.py:39
  188.5 8.5 %collective-permute-start.23 = (f32[1,512,128]{2,1,0:T(8,128)S(1)}, f32[1,512,128]{2,1,0:T(8,128)S(1)}, u32[]{:S(2)}, u32[]{:S(2)}) collective-permute-start(f32[1,512,128]{2,1,0:T(8,128)S(1)} %get-tuple-element.130), channel_id=1, source_target_pairs={{1,0},{2,1},{3,2},{5,4},{6,5},{7,6},{9,8},{10,9},{11,10},{13,12},{... | collective-permute-start | bytes 786440 | tf_op jit(solution)/shard_map/ppermute | solution.py:40
  189.8 8.3 %collective-permute-start.24 = (f32[1,512,128]{2,1,0:T(8,128)S(1)}, f32[1,512,128]{2,1,0:T(8,128)S(1)}, u32[]{:S(2)}, u32[]{:S(2)}) collective-permute-start(f32[1,512,128]{2,1,0:T(8,128)S(1)} %get-tuple-element.129), channel_id=1, source_target_pairs={{0,1},{1,2},{2,3},{4,5},{5,6},{6,7},{8,9},{9,10},{10,11},{12,13},{... | collective-permute-start | bytes 786440 | tf_op jit(solution)/shard_map/ppermute | solution.py:39
  199.3 8.5 %collective-permute-start.25 = (f32[1,512,128]{2,1,0:T(8,128)S(1)}, f32[1,512,128]{2,1,0:T(8,128)S(1)}, u32[]{:S(2)}, u32[]{:S(2)}) collective-permute-start(f32[1,512,128]{2,1,0:T(8,128)S(1)} %get-tuple-element.128), channel_id=1, source_target_pairs={{1,0},{2,1},{3,2},{5,4},{6,5},{7,6},{9,8},{10,9},{11,10},{13,12},{... | collective-permute-start | bytes 786440 | tf_op jit(solution)/shard_map/ppermute | solution.py:40
  200.6 8.3 %collective-permute-start.26 = (f32[1,512,128]{2,1,0:T(8,128)S(1)}, f32[1,512,128]{2,1,0:T(8,128)S(1)}, u32[]{:S(2)}, u32[]{:S(2)}) collective-permute-start(f32[1,512,128]{2,1,0:T(8,128)S(1)} %get-tuple-element.127), channel_id=1, source_target_pairs={{0,1},{1,2},{2,3},{4,5},{5,6},{6,7},{8,9},{9,10},{10,11},{12,13},{... | collective-permute-start | bytes 786440 | tf_op jit(solution)/shard_map/ppermute | solution.py:39
  210.3 8.5 %collective-permute-start.27 = (f32[1,512,128]{2,1,0:T(8,128)S(1)}, f32[1,512,128]{2,1,0:T(8,128)S(1)}, u32[]{:S(2)}, u32[]{:S(2)}) collective-permute-start(f32[1,512,128]{2,1,0:T(8,128)S(1)} %get-tuple-element.126), channel_id=1, source_target_pairs={{1,0},{2,1},{3,2},{5,4},{6,5},{7,6},{9,8},{10,9},{11,10},{13,12},{... | collective-permute-start | bytes 786440 | tf_op jit(solution)/shard_map/ppermute | solution.py:40
  211.6 8.3 %collective-permute-start.28 = (f32[1,512,128]{2,1,0:T(8,128)S(1)}, f32[1,512,128]{2,1,0:T(8,128)S(1)}, u32[]{:S(2)}, u32[]{:S(2)}) collective-permute-start(f32[1,512,128]{2,1,0:T(8,128)S(1)} %get-tuple-element.125), channel_id=1, source_target_pairs={{0,1},{1,2},{2,3},{4,5},{5,6},{6,7},{8,9},{9,10},{10,11},{12,13},{... | collective-permute-start | bytes 786440 | tf_op jit(solution)/shard_map/ppermute | solution.py:39
  221.1 8.7 %collective-permute-start.29 = (f32[1,512,128]{2,1,0:T(8,128)S(1)}, f32[1,512,128]{2,1,0:T(8,128)S(1)}, u32[]{:S(2)}, u32[]{:S(2)}) collective-permute-start(f32[1,512,128]{2,1,0:T(8,128)S(1)} %get-tuple-element.124), channel_id=1, source_target_pairs={{1,0},{2,1},{3,2},{5,4},{6,5},{7,6},{9,8},{10,9},{11,10},{13,12},{... | collective-permute-start | bytes 786440 | tf_op jit(solution)/shard_map/ppermute | solution.py:40
  222.4 8.3 %collective-permute-start.30 = (f32[1,512,128]{2,1,0:T(8,128)S(1)}, f32[1,512,128]{2,1,0:T(8,128)S(1)}, u32[]{:S(2)}, u32[]{:S(2)}) collective-permute-start(f32[1,512,128]{2,1,0:T(8,128)S(1)} %get-tuple-element.123), channel_id=1, source_target_pairs={{0,1},{1,2},{2,3},{4,5},{5,6},{6,7},{8,9},{9,10},{10,11},{12,13},{... | collective-permute-start | bytes 786440 | tf_op jit(solution)/shard_map/ppermute | solution.py:39
  232.0 8.5 %collective-permute-start.31 = (f32[1,512,128]{2,1,0:T(8,128)S(1)}, f32[1,512,128]{2,1,0:T(8,128)S(1)}, u32[]{:S(2)}, u32[]{:S(2)}) collective-permute-start(f32[1,512,128]{2,1,0:T(8,128)S(1)} %get-tuple-element.122), channel_id=1, source_target_pairs={{1,0},{2,1},{3,2},{5,4},{6,5},{7,6},{9,8},{10,9},{11,10},{13,12},{... | collective-permute-start | bytes 786440 | tf_op jit(solution)/shard_map/ppermute | solution.py:40
  233.3 8.3 %collective-permute-start.32 = (f32[1,512,128]{2,1,0:T(8,128)S(1)}, f32[1,512,128]{2,1,0:T(8,128)S(1)}, u32[]{:S(2)}, u32[]{:S(2)}) collective-permute-start(f32[1,512,128]{2,1,0:T(8,128)S(1)} %get-tuple-element.121), channel_id=1, source_target_pairs={{0,1},{1,2},{2,3},{4,5},{5,6},{6,7},{8,9},{9,10},{10,11},{12,13},{... | collective-permute-start | bytes 786440 | tf_op jit(solution)/shard_map/ppermute | solution.py:39
  242.8 8.5 %collective-permute-start.33 = (f32[1,512,128]{2,1,0:T(8,128)S(1)}, f32[1,512,128]{2,1,0:T(8,128)S(1)}, u32[]{:S(2)}, u32[]{:S(2)}) collective-permute-start(f32[1,512,128]{2,1,0:T(8,128)S(1)} %get-tuple-element.120), channel_id=1, source_target_pairs={{1,0},{2,1},{3,2},{5,4},{6,5},{7,6},{9,8},{10,9},{11,10},{13,12},{... | collective-permute-start | bytes 786440 | tf_op jit(solution)/shard_map/ppermute | solution.py:40
  244.1 8.3 %collective-permute-start.34 = (f32[1,512,128]{2,1,0:T(8,128)S(1)}, f32[1,512,128]{2,1,0:T(8,128)S(1)}, u32[]{:S(2)}, u32[]{:S(2)}) collective-permute-start(f32[1,512,128]{2,1,0:T(8,128)S(1)} %get-tuple-element.119), channel_id=1, source_target_pairs={{0,1},{1,2},{2,3},{4,5},{5,6},{6,7},{8,9},{9,10},{10,11},{12,13},{... | collective-permute-start | bytes 786440 | tf_op jit(solution)/shard_map/ppermute | solution.py:39
  253.6 8.5 %collective-permute-start.35 = (f32[1,512,128]{2,1,0:T(8,128)S(1)}, f32[1,512,128]{2,1,0:T(8,128)S(1)}, u32[]{:S(2)}, u32[]{:S(2)}) collective-permute-start(f32[1,512,128]{2,1,0:T(8,128)S(1)} %get-tuple-element.118), channel_id=1, source_target_pairs={{1,0},{2,1},{3,2},{5,4},{6,5},{7,6},{9,8},{10,9},{11,10},{13,12},{... | collective-permute-start | bytes 786440 | tf_op jit(solution)/shard_map/ppermute | solution.py:40
  264.4 8.6 %collective-permute-start.37 = (f32[1,512,128]{2,1,0:T(8,128)S(1)}, f32[1,512,128]{2,1,0:T(8,128)S(1)}, u32[]{:S(2)}, u32[]{:S(2)}) collective-permute-start(f32[1,512,128]{2,1,0:T(8,128)S(1)} %get-tuple-element.116), channel_id=1, source_target_pairs={{1,0},{2,1},{3,2},{5,4},{6,5},{7,6},{9,8},{10,9},{11,10},{13,12},{... | collective-permute-start | bytes 786440 | tf_op jit(solution)/shard_map/ppermute | solution.py:40
  275.6 8.5 %collective-permute-start.39 = (f32[1,512,128]{2,1,0:T(8,128)S(1)}, f32[1,512,128]{2,1,0:T(8,128)S(1)}, u32[]{:S(2)}, u32[]{:S(2)}) collective-permute-start(f32[1,512,128]{2,1,0:T(8,128)S(1)} %get-tuple-element.114), channel_id=1, source_target_pairs={{1,0},{2,1},{3,2},{5,4},{6,5},{7,6},{9,8},{10,9},{11,10},{13,12},{... | collective-permute-start | bytes 786440 | tf_op jit(solution)/shard_map/ppermute | solution.py:40
  286.4 8.5 %collective-permute-start.41 = (f32[1,512,128]{2,1,0:T(8,128)S(1)}, f32[1,512,128]{2,1,0:T(8,128)S(1)}, u32[]{:S(2)}, u32[]{:S(2)}) collective-permute-start(f32[1,512,128]{2,1,0:T(8,128)S(1)} %get-tuple-element.112), channel_id=1, source_target_pairs={{1,0},{2,1},{3,2},{5,4},{6,5},{7,6},{9,8},{10,9},{11,10},{13,12},{... | collective-permute-start | bytes 786440 | tf_op jit(solution)/shard_map/ppermute | solution.py:40
  297.2 8.5 %collective-permute-start.43 = (f32[1,512,128]{2,1,0:T(8,128)S(1)}, f32[1,512,128]{2,1,0:T(8,128)S(1)}, u32[]{:S(2)}, u32[]{:S(2)}) collective-permute-start(f32[1,512,128]{2,1,0:T(8,128)S(1)} %get-tuple-element.110), channel_id=1, source_target_pairs={{1,0},{2,1},{3,2},{5,4},{6,5},{7,6},{9,8},{10,9},{11,10},{13,12},{... | collective-permute-start | bytes 786440 | tf_op jit(solution)/shard_map/ppermute | solution.py:40
  308.0 8.9 %collective-permute-start.45 = (f32[1,512,128]{2,1,0:T(8,128)S(1)}, f32[1,512,128]{2,1,0:T(8,128)S(1)}, u32[]{:S(2)}, u32[]{:S(2)}) collective-permute-start(f32[1,512,128]{2,1,0:T(8,128)S(1)} %get-tuple-element.108), channel_id=1, source_target_pairs={{1,0},{2,1},{3,2},{5,4},{6,5},{7,6},{9,8},{10,9},{11,10},{13,12},{... | collective-permute-start | bytes 786440 | tf_op jit(solution)/shard_map/ppermute | solution.py:40
  318.8 8.5 %collective-permute-start.47 = (f32[1,512,128]{2,1,0:T(8,128)S(1)}, f32[1,512,128]{2,1,0:T(8,128)S(1)}, u32[]{:S(2)}, u32[]{:S(2)}) collective-permute-start(f32[1,512,128]{2,1,0:T(8,128)S(1)} %get-tuple-element.106), channel_id=1, source_target_pairs={{1,0},{2,1},{3,2},{5,4},{6,5},{7,6},{9,8},{10,9},{11,10},{13,12},{... | collective-permute-start | bytes 786440 | tf_op jit(solution)/shard_map/ppermute | solution.py:40
  329.6 8.5 %collective-permute-start.49 = (f32[1,512,128]{2,1,0:T(8,128)S(1)}, f32[1,512,128]{2,1,0:T(8,128)S(1)}, u32[]{:S(2)}, u32[]{:S(2)}) collective-permute-start(f32[1,512,128]{2,1,0:T(8,128)S(1)} %get-tuple-element.104), channel_id=1, source_target_pairs={{1,0},{2,1},{3,2},{5,4},{6,5},{7,6},{9,8},{10,9},{11,10},{13,12},{... | collective-permute-start | bytes 786440 | tf_op jit(solution)/shard_map/ppermute | solution.py:40
  340.7 8.5 %collective-permute-start.51 = (f32[1,512,128]{2,1,0:T(8,128)S(1)}, f32[1,512,128]{2,1,0:T(8,128)S(1)}, u32[]{:S(2)}, u32[]{:S(2)}) collective-permute-start(f32[1,512,128]{2,1,0:T(8,128)S(1)} %get-tuple-element.102), channel_id=1, source_target_pairs={{1,0},{2,1},{3,2},{5,4},{6,5},{7,6},{9,8},{10,9},{11,10},{13,12},{... | collective-permute-start | bytes 786440 | tf_op jit(solution)/shard_map/ppermute | solution.py:40
  351.5 8.5 %collective-permute-start.53 = (f32[1,512,128]{2,1,0:T(8,128)S(1)}, f32[1,512,128]{2,1,0:T(8,128)S(1)}, u32[]{:S(2)}, u32[]{:S(2)}) collective-permute-start(f32[1,512,128]{2,1,0:T(8,128)S(1)} %get-tuple-element.100), channel_id=1, source_target_pairs={{1,0},{2,1},{3,2},{5,4},{6,5},{7,6},{9,8},{10,9},{11,10},{13,12},{... | collective-permute-start | bytes 786440 | tf_op jit(solution)/shard_map/ppermute | solution.py:40
  362.3 8.5 %collective-permute-start.55 = (f32[1,512,128]{2,1,0:T(8,128)S(1)}, f32[1,512,128]{2,1,0:T(8,128)S(1)}, u32[]{:S(2)}, u32[]{:S(2)}) collective-permute-start(f32[1,512,128]{2,1,0:T(8,128)S(1)} %get-tuple-element.98), channel_id=1, source_target_pairs={{1,0},{2,1},{3,2},{5,4},{6,5},{7,6},{9,8},{10,9},{11,10},{13,12},{... | collective-permute-start | bytes 786440 | tf_op jit(solution)/shard_map/ppermute | solution.py:40
  373.2 8.5 %collective-permute-start.57 = (f32[1,512,128]{2,1,0:T(8,128)S(1)}, f32[1,512,128]{2,1,0:T(8,128)S(1)}, u32[]{:S(2)}, u32[]{:S(2)}) collective-permute-start(f32[1,512,128]{2,1,0:T(8,128)S(1)} %get-tuple-element.96), channel_id=1, source_target_pairs={{1,0},{2,1},{3,2},{5,4},{6,5},{7,6},{9,8},{10,9},{11,10},{13,12},{... | collective-permute-start | bytes 786440 | tf_op jit(solution)/shard_map/ppermute | solution.py:40
  384.0 8.5 %collective-permute-start.59 = (f32[1,512,128]{2,1,0:T(8,128)S(1)}, f32[1,512,128]{2,1,0:T(8,128)S(1)}, u32[]{:S(2)}, u32[]{:S(2)}) collective-permute-start(f32[1,512,128]{2,1,0:T(8,128)S(1)} %get-tuple-element.94), channel_id=1, source_target_pairs={{1,0},{2,1},{3,2},{5,4},{6,5},{7,6},{9,8},{10,9},{11,10},{13,12},{... | collective-permute-start | bytes 786440 | tf_op jit(solution)/shard_map/ppermute | solution.py:40
  394.8 8.7 %collective-permute-start.61 = (f32[1,512,128]{2,1,0:T(8,128)S(1)}, f32[1,512,128]{2,1,0:T(8,128)S(1)}, u32[]{:S(2)}, u32[]{:S(2)}) collective-permute-start(f32[1,512,128]{2,1,0:T(8,128)S(1)} %get-tuple-element.92), channel_id=1, source_target_pairs={{1,0},{2,1},{3,2},{5,4},{6,5},{7,6},{9,8},{10,9},{11,10},{13,12},{... | collective-permute-start | bytes 786440 | tf_op jit(solution)/shard_map/ppermute | solution.py:40
  405.8 8.5 %collective-permute-start.63 = (f32[1,512,128]{2,1,0:T(8,128)S(1)}, f32[1,512,128]{2,1,0:T(8,128)S(1)}, u32[]{:S(2)}, u32[]{:S(2)}) collective-permute-start(f32[1,512,128]{2,1,0:T(8,128)S(1)} %get-tuple-element.90), channel_id=1, source_target_pairs={{1,0},{2,1},{3,2},{5,4},{6,5},{7,6},{9,8},{10,9},{11,10},{13,12},{... | collective-permute-start | bytes 786440 | tf_op jit(solution)/shard_map/ppermute | solution.py:40
  416.6 8.5 %collective-permute-start.65 = (f32[1,512,128]{2,1,0:T(8,128)S(1)}, f32[1,512,128]{2,1,0:T(8,128)S(1)}, u32[]{:S(2)}, u32[]{:S(2)}) collective-permute-start(f32[1,512,128]{2,1,0:T(8,128)S(1)} %get-tuple-element.88), channel_id=1, source_target_pairs={{1,0},{2,1},{3,2},{5,4},{6,5},{7,6},{9,8},{10,9},{11,10},{13,12},{... | collective-permute-start | bytes 786440 | tf_op jit(solution)/shard_map/ppermute | solution.py:40
  427.4 8.5 %collective-permute-start.67 = (f32[1,512,128]{2,1,0:T(8,128)S(1)}, f32[1,512,128]{2,1,0:T(8,128)S(1)}, u32[]{:S(2)}, u32[]{:S(2)}) collective-permute-start(f32[1,512,128]{2,1,0:T(8,128)S(1)} %get-tuple-element.86), channel_id=1, source_target_pairs={{1,0},{2,1},{3,2},{5,4},{6,5},{7,6},{9,8},{10,9},{11,10},{13,12},{... | collective-permute-start | bytes 786440 | tf_op jit(solution)/shard_map/ppermute | solution.py:40
  438.2 8.5 %collective-permute-start.69 = (f32[1,512,128]{2,1,0:T(8,128)S(1)}, f32[1,512,128]{2,1,0:T(8,128)S(1)}, u32[]{:S(2)}, u32[]{:S(2)}) collective-permute-start(f32[1,512,128]{2,1,0:T(8,128)S(1)} %get-tuple-element.84), channel_id=1, source_target_pairs={{1,0},{2,1},{3,2},{5,4},{6,5},{7,6},{9,8},{10,9},{11,10},{13,12},{... | collective-permute-start | bytes 786440 | tf_op jit(solution)/shard_map/ppermute | solution.py:40
  449.1 8.5 %collective-permute-start.71 = (f32[1,512,128]{2,1,0:T(8,128)S(1)}, f32[1,512,128]{2,1,0:T(8,128)S(1)}, u32[]{:S(2)}, u32[]{:S(2)}) collective-permute-start(f32[1,512,128]{2,1,0:T(8,128)S(1)} %get-tuple-element.82), channel_id=1, source_target_pairs={{1,0},{2,1},{3,2},{5,4},{6,5},{7,6},{9,8},{10,9},{11,10},{13,12},{... | collective-permute-start | bytes 786440 | tf_op jit(solution)/shard_map/ppermute | solution.py:40
  459.9 8.5 %collective-permute-start.73 = (f32[1,512,128]{2,1,0:T(8,128)S(1)}, f32[1,512,128]{2,1,0:T(8,128)S(1)}, u32[]{:S(2)}, u32[]{:S(2)}) collective-permute-start(f32[1,512,128]{2,1,0:T(8,128)S(1)} %get-tuple-element.80), channel_id=1, source_target_pairs={{1,0},{2,1},{3,2},{5,4},{6,5},{7,6},{9,8},{10,9},{11,10},{13,12},{... | collective-permute-start | bytes 786440 | tf_op jit(solution)/shard_map/ppermute | solution.py:40
  (34 other events, 566.4 us)
Sparse Core Ops, SparseCore 0:
  473.7 108.5 all-reduce.38
